TPU v7x, 512 devices: a whole 4x4x16 slice. The times are simulated.
512 devices in a mesh: dp: 16 (over z), ctx: 16 (over x_lo, y, core), head: 2 (over x_hi).
Axes of the slice: x: 4 (x_hi: 2, x_lo: 2; x = x_hi * 2 + x_lo), y: 4, z: 16, core: 2. Of those that a mesh axis runs over, the one named last changes fastest.
Arguments:
- queries: bfloat16 [32768, 4096], P(('dp', 'ctx'), 'head'), parts along dimension 0, may hold values from -18 to 18
- keys: bfloat16 [32768, 1024], P(('dp', 'ctx'), 'head'), parts along dimension 0, may hold values from -18 to 18
- values: bfloat16 [32768, 1024], P(('dp', 'ctx'), 'head'), parts along dimension 0, may hold values from -6 to 6
- doc_lengths: int32 [256], P('dp'), parts along dimension 0, may hold values from 1 to 1024, 2048 in all
- owner_map: int32 [256, 16], P('dp'), parts along dimension 0, may hold values from 0 to 15, each once within a row
Outputs:
- attended: bfloat16 [32768, 4096], P(('dp', 'ctx'), 'head'), parts along dimension 0
There are 16 independent parts, one for each index of `dp`. A program takes and returns all parts, laid end to end along the dimension named above; each array names one. Nothing has to cross between parts.
Inputs may be any that keep to these rules, and one draw needn't show every extreme that they name: Each row of owner_map names every ctx index exactly once. `doc_lengths`: the lengths sum to 2048; the longest is exactly 1024.
All inputs are finite; a program needn't handle non-finite values.
Results may differ from a plain program's by a relative error of at most 0.003.
Values may be sent and summed in bfloat16 or wider, within the bound.
No kernel may reach another device: no remote copies, remote signals or barrier semaphores. Data moves between devices by JAX's collectives and lax.ppermute only.
A program may use at most 64 MiB of HBM per device.

v0:
```python
from functools import partial
import math

import jax
import jax.numpy as jnp
from jax import lax
from jax.sharding import PartitionSpec as P

HEAD_SIZE = 128


MASKED = -1e30


def passed_along(value, axis, steps):
    count = lax.axis_size(axis)
    pairs = [(source, (source + steps) % count) for source in range(count)]
    return lax.ppermute(value, axis, pairs)


def doc_index(doc_ends, positions):
    return jnp.sum((doc_ends[None, :] <= positions[:, None]).astype(jnp.int32), axis=1)


def update(query_tile, key_rows, value_rows, visible, state):
    running_max, totals, accum_sum = state
    scores = jnp.einsum(
        "qkgd,tkd->kgqt", query_tile, key_rows, preferred_element_type=jnp.float32
    ) * (1.0 / math.sqrt(HEAD_SIZE))
    scores = jnp.where(visible[None, None], scores, MASKED)
    new_max = jnp.maximum(running_max, jnp.max(scores, axis=-1))
    shrink = jnp.exp(running_max - new_max)
    weights = jnp.where(visible[None, None], jnp.exp(scores - new_max[..., None]), 0.0)
    totals = totals * shrink + jnp.sum(weights, axis=-1)
    accum_sum = accum_sum * shrink[..., None] + jnp.einsum(
        "kgqt,tkd->kgqd",
        weights.astype(jnp.bfloat16),
        value_rows,
        preferred_element_type=jnp.float32,
    )
    return (new_max, totals, accum_sum)


def unchanged(state):
    return state


def circulate(
    query_heads, positions, query_docs, packed, advance, direction, doc_ends, my_index, cycle_size
):
    tok_rows, kv_heads, query_group_size = (
        query_heads.shape[0],
        query_heads.shape[1],
        query_heads.shape[2],
    )
    tile_rows = min(128, tok_rows)
    tile_count = tok_rows // tile_rows
    initial = tuple(
        (
            (
                jnp.full((kv_heads, query_group_size, tile_rows), MASKED, jnp.float32),
                jnp.zeros((kv_heads, query_group_size, tile_rows), jnp.float32),
                jnp.zeros((kv_heads, query_group_size, tile_rows, HEAD_SIZE), jnp.float32),
            )
            for tile_index in range(tile_count)
        )
    )

    def absorb(states, packed_now, source):
        key_pos = source * tok_rows + jnp.arange(tok_rows, dtype=jnp.int32)
        key_docs = doc_index(doc_ends, key_pos)
        key_rows = packed_now[0].reshape(tok_rows, kv_heads, HEAD_SIZE)
        value_rows = packed_now[1].reshape(tok_rows, kv_heads, HEAD_SIZE)
        visible = (key_pos[None, :] <= positions[:, None]) & (
            key_docs[None, :] == query_docs[:, None]
        )
        renewed = [
            lax.cond(
                jnp.any(visible),
                partial(update, query_heads, key_rows, value_rows, visible),
                unchanged,
                states[0],
            )
        ]
        return tuple(renewed)

    states = absorb(initial, packed, my_index)

    def turn(turn_index, carried):
        states_now, packed_now = carried
        packed_now = advance(packed_now)
        source = (my_index - direction * turn_index) % cycle_size
        return (absorb(states_now, packed_now, source), packed_now)

    states, packed = lax.fori_loop(1, cycle_size, turn, (states, packed))
    return jnp.concatenate(
        [accum_sum / totals[..., None] for running_max, totals, accum_sum in states], axis=2
    )


def attend(row_data, positions, keys, values, doc_ends, my_index, cycle_size):
    tok_rows = row_data.shape[0]
    kv_heads = keys.shape[1] // HEAD_SIZE
    query_group_size = row_data.shape[1] // keys.shape[1]
    query_heads = row_data.reshape(tok_rows, kv_heads, query_group_size, HEAD_SIZE)
    query_docs = doc_index(doc_ends, positions)

    def around_move(packed_now):
        return passed_along(packed_now, "ctx", 1)

    mixed = circulate(
        query_heads,
        positions,
        query_docs,
        jnp.stack([keys, values]),
        around_move,
        1,
        doc_ends,
        my_index,
        cycle_size,
    )
    return mixed.transpose(2, 0, 1, 3).reshape(tok_rows, -1).astype(jnp.bfloat16)


def body(queries, keys, values, doc_lengths, owner_map):
    cycle_size = lax.axis_size("ctx")
    my_index = lax.axis_index("ctx")
    tok_rows = queries.shape[0]
    block_rows = tok_rows // cycle_size
    doc_ends = jnp.cumsum(doc_lengths)
    slot_ids = jnp.arange(cycle_size, dtype=jnp.int32)
    chosen_block = jnp.sum(
        slot_ids[None, None, :]
        * (owner_map[None, :, :] == slot_ids[:, None, None]).astype(jnp.int32),
        axis=2,
    )
    picker = (owner_map[my_index][None, :] == slot_ids[:, None]).astype(jnp.bfloat16)
    blocks = queries.reshape(cycle_size, block_rows, queries.shape[1])
    arrived = lax.all_to_all(
        jnp.einsum("jb,brf->jrf", picker, blocks, preferred_element_type=jnp.float32).astype(
            jnp.bfloat16
        ),
        "ctx",
        split_axis=0,
        concat_axis=0,
        tiled=True,
    )
    row_data = arrived.reshape(tok_rows, queries.shape[1])
    positions = (
        slot_ids[:, None] * tok_rows
        + chosen_block[my_index][:, None] * block_rows
        + jnp.arange(block_rows, dtype=jnp.int32)[None, :]
    ).reshape(-1)
    return attend(row_data, positions, keys, values, doc_ends, my_index, cycle_size)


def solution(mesh):
    placed = (
        P(("dp", "ctx"), "head"),
        P(("dp", "ctx"), "head"),
        P(("dp", "ctx"), "head"),
        P("dp"),
        P("dp", None),
    )
    return jax.shard_map(
        body, mesh=mesh, in_specs=placed, out_specs=P(("dp", "ctx"), "head"), check_vma=False
    )
```

profile of v0, /device:TPU:2, one launch (start us, length us, event | category | flops | bytes accessed | tf_op | source)
XLA Modules:
  0.0 239.2 jit_solution(17697544587284137411)
XLA Ops:
  2.8 9.4 %all-to-all-start = ((bf16[16,8,2048]{2,1,0:T(8,128)(2,1)}), bf16[16,8,2048]{2,1,0:T(8,128)(2,1)S(1)}, u32[]{:S(2)}, u32[]{:S(2)}) async-start(bf16[16,8,2048]{2,1,0:T(8,128)(2,1)} %copy.49), calls=%async_computation | async-start | bytes 1048576 | tf_op jit(solution)/shard_map/all_to_all | solution.py:139
  17.7 4.1 %all-to-all-done = bf16[16,8,2048]{2,1,0:T(8,128)(2,1)S(1)} async-done(((bf16[16,8,2048]{2,1,0:T(8,128)(2,1)}), bf16[16,8,2048]{2,1,0:T(8,128)(2,1)S(1)}, u32[]{:S(2)}, u32[]{:S(2)}) %all-to-all-start) | async-done | bytes 524320 | tf_op jit(solution)/shard_map/all_to_all | solution.py:139
  22.9 4.6 %conditional.2 = (f32[4,4,128]{2,1,0:T(4,128)}, f32[4,4,128]{2,1,0:T(4,128)S(1)}, f32[4,4,128,128]{3,2,1,0:T(8,128)S(1)}) conditional(s32[]{:T(128)} %convert_element_type.51, () %tuple.42, (pred[128,128]{0,1:T(8,128)(4,1)S(1)}, bf16[128,512]{1,0:T(8,128)(2,1)S(1)}, bf16[128,4,4,128]{3,2,1,0:T(4,128)(2,1)S(1)}, bf16[128,512]{1,0:T(8,128)(2,1)S(1)}) %tuple.91), branch_computations={%region_5.6_spmd, %region_6.9_spmd} | conditional | flops 136847360 | bytes 5775440 | solution.py:78
  27.4 209.8 %while.22 = (s32[]{:T(128)}, f32[4,4,128]{2,1,0:T(4,128)}, f32[4,4,128]{2,1,0:T(4,128)S(1)}, f32[4,4,128,128]{3,2,1,0:T(8,128)S(1)}, bf16[2,128,512]{1,2,0:T(8,1...) while((s32[]{:T(128)}, f32[4,4,128]{2,1,0:T(4,128)}, ...), condition=%wide.region_16.17_spmd.clone, body=%wide.region_9.16_spmd.clone.sunk | while | flops 137177232 | bytes 8328748 | solution.py:95
  31.1 6.4 %collective-permute-done = bf16[2,128,512]{1,2,0:T(8,128)(2,1)S(1)} collective-permute-done((bf16[2,128,512]{1,2,0:T(8,128)(2,1)}, bf16[2,128,512]{1,2,0:T(8,128)(2,1)S(1)}, u32[]{:S(2)}, u32[]{:S(2)}) %collective-permute-start) | collective-permute-done | bytes 262176 | tf_op jit(solution)/shard_map/while/body/eval_jaxpr/ppermute | solution.py:18
  45.0 6.4 %collective-permute-done = bf16[2,128,512]{1,2,0:T(8,128)(2,1)S(1)} collective-permute-done((bf16[2,128,512]{1,2,0:T(8,128)(2,1)}, bf16[2,128,512]{1,2,0:T(8,128)(2,1)S(1)}, u32[]{:S(2)}, u32[]{:S(2)}) %collective-permute-start) | collective-permute-done | bytes 262176 | tf_op jit(solution)/shard_map/while/body/eval_jaxpr/ppermute | solution.py:18
  59.0 6.4 %collective-permute-done = bf16[2,128,512]{1,2,0:T(8,128)(2,1)S(1)} collective-permute-done((bf16[2,128,512]{1,2,0:T(8,128)(2,1)}, bf16[2,128,512]{1,2,0:T(8,128)(2,1)S(1)}, u32[]{:S(2)}, u32[]{:S(2)}) %collective-permute-start) | collective-permute-done | bytes 262176 | tf_op jit(solution)/shard_map/while/body/eval_jaxpr/ppermute | solution.py:18
  65.4 3.3 %conditional.5 = ((f32[4,4,128]{2,1,0:T(4,128)}, f32[4,4,128]{2,1,0:T(4,128)S(1)}, f32[4,4,128,128]{3,2,1,0:T(8,128)S(1)})) conditional(s32[]{:T(128)} %convert_element_type.72, (f32[4,4,128]{2,1,0:T(4,128)}, f32[4,4,128]{2,1,0:T(4,128)S(1)}, f32[4,4,128,128]{3,2,1,0:T(8,128)S(1)}) %tuple.77, (pred[128,128]{0,1:T(8,128)(4,1)S(1)}, ...), branch_computations={%region_12.12_spmd, %region_13.15_spmd} | conditional | flops 137105408 | bytes 6733856 | solution.py:78
  73.0 6.4 %collective-permute-done = bf16[2,128,512]{1,2,0:T(8,128)(2,1)S(1)} collective-permute-done((bf16[2,128,512]{1,2,0:T(8,128)(2,1)}, bf16[2,128,512]{1,2,0:T(8,128)(2,1)S(1)}, u32[]{:S(2)}, u32[]{:S(2)}) %collective-permute-start) | collective-permute-done | bytes 262176 | tf_op jit(solution)/shard_map/while/body/eval_jaxpr/ppermute | solution.py:18
  79.4 3.3 %conditional.5 = ((f32[4,4,128]{2,1,0:T(4,128)}, f32[4,4,128]{2,1,0:T(4,128)S(1)}, f32[4,4,128,128]{3,2,1,0:T(8,128)S(1)})) conditional(s32[]{:T(128)} %convert_element_type.72, (f32[4,4,128]{2,1,0:T(4,128)}, f32[4,4,128]{2,1,0:T(4,128)S(1)}, f32[4,4,128,128]{3,2,1,0:T(8,128)S(1)}) %tuple.77, (pred[128,128]{0,1:T(8,128)(4,1)S(1)}, ...), branch_computations={%region_12.12_spmd, %region_13.15_spmd} | conditional | flops 137105408 | bytes 6733856 | solution.py:78
  87.0 6.4 %collective-permute-done = bf16[2,128,512]{1,2,0:T(8,128)(2,1)S(1)} collective-permute-done((bf16[2,128,512]{1,2,0:T(8,128)(2,1)}, bf16[2,128,512]{1,2,0:T(8,128)(2,1)S(1)}, u32[]{:S(2)}, u32[]{:S(2)}) %collective-permute-start) | collective-permute-done | bytes 262176 | tf_op jit(solution)/shard_map/while/body/eval_jaxpr/ppermute | solution.py:18
  93.4 3.3 %conditional.5 = ((f32[4,4,128]{2,1,0:T(4,128)}, f32[4,4,128]{2,1,0:T(4,128)S(1)}, f32[4,4,128,128]{3,2,1,0:T(8,128)S(1)})) conditional(s32[]{:T(128)} %convert_element_type.72, (f32[4,4,128]{2,1,0:T(4,128)}, f32[4,4,128]{2,1,0:T(4,128)S(1)}, f32[4,4,128,128]{3,2,1,0:T(8,128)S(1)}) %tuple.77, (pred[128,128]{0,1:T(8,128)(4,1)S(1)}, ...), branch_computations={%region_12.12_spmd, %region_13.15_spmd} | conditional | flops 137105408 | bytes 6733856 | solution.py:78
  101.0 6.4 %collective-permute-done = bf16[2,128,512]{1,2,0:T(8,128)(2,1)S(1)} collective-permute-done((bf16[2,128,512]{1,2,0:T(8,128)(2,1)}, bf16[2,128,512]{1,2,0:T(8,128)(2,1)S(1)}, u32[]{:S(2)}, u32[]{:S(2)}) %collective-permute-start) | collective-permute-done | bytes 262176 | tf_op jit(solution)/shard_map/while/body/eval_jaxpr/ppermute | solution.py:18
  107.4 3.3 %conditional.5 = ((f32[4,4,128]{2,1,0:T(4,128)}, f32[4,4,128]{2,1,0:T(4,128)S(1)}, f32[4,4,128,128]{3,2,1,0:T(8,128)S(1)})) conditional(s32[]{:T(128)} %convert_element_type.72, (f32[4,4,128]{2,1,0:T(4,128)}, f32[4,4,128]{2,1,0:T(4,128)S(1)}, f32[4,4,128,128]{3,2,1,0:T(8,128)S(1)}) %tuple.77, (pred[128,128]{0,1:T(8,128)(4,1)S(1)}, ...), branch_computations={%region_12.12_spmd, %region_13.15_spmd} | conditional | flops 137105408 | bytes 6733856 | solution.py:78
  115.0 6.4 %collective-permute-done = bf16[2,128,512]{1,2,0:T(8,128)(2,1)S(1)} collective-permute-done((bf16[2,128,512]{1,2,0:T(8,128)(2,1)}, bf16[2,128,512]{1,2,0:T(8,128)(2,1)S(1)}, u32[]{:S(2)}, u32[]{:S(2)}) %collective-permute-start) | collective-permute-done | bytes 262176 | tf_op jit(solution)/shard_map/while/body/eval_jaxpr/ppermute | solution.py:18
  121.4 3.3 %conditional.5 = ((f32[4,4,128]{2,1,0:T(4,128)}, f32[4,4,128]{2,1,0:T(4,128)S(1)}, f32[4,4,128,128]{3,2,1,0:T(8,128)S(1)})) conditional(s32[]{:T(128)} %convert_element_type.72, (f32[4,4,128]{2,1,0:T(4,128)}, f32[4,4,128]{2,1,0:T(4,128)S(1)}, f32[4,4,128,128]{3,2,1,0:T(8,128)S(1)}) %tuple.77, (pred[128,128]{0,1:T(8,128)(4,1)S(1)}, ...), branch_computations={%region_12.12_spmd, %region_13.15_spmd} | conditional | flops 137105408 | bytes 6733856 | solution.py:78
  129.0 6.4 %collective-permute-done = bf16[2,128,512]{1,2,0:T(8,128)(2,1)S(1)} collective-permute-done((bf16[2,128,512]{1,2,0:T(8,128)(2,1)}, bf16[2,128,512]{1,2,0:T(8,128)(2,1)S(1)}, u32[]{:S(2)}, u32[]{:S(2)}) %collective-permute-start) | collective-permute-done | bytes 262176 | tf_op jit(solution)/shard_map/while/body/eval_jaxpr/ppermute | solution.py:18
  135.4 3.3 %conditional.5 = ((f32[4,4,128]{2,1,0:T(4,128)}, f32[4,4,128]{2,1,0:T(4,128)S(1)}, f32[4,4,128,128]{3,2,1,0:T(8,128)S(1)})) conditional(s32[]{:T(128)} %convert_element_type.72, (f32[4,4,128]{2,1,0:T(4,128)}, f32[4,4,128]{2,1,0:T(4,128)S(1)}, f32[4,4,128,128]{3,2,1,0:T(8,128)S(1)}) %tuple.77, (pred[128,128]{0,1:T(8,128)(4,1)S(1)}, ...), branch_computations={%region_12.12_spmd, %region_13.15_spmd} | conditional | flops 137105408 | bytes 6733856 | solution.py:78
  142.9 6.4 %collective-permute-done = bf16[2,128,512]{1,2,0:T(8,128)(2,1)S(1)} collective-permute-done((bf16[2,128,512]{1,2,0:T(8,128)(2,1)}, bf16[2,128,512]{1,2,0:T(8,128)(2,1)S(1)}, u32[]{:S(2)}, u32[]{:S(2)}) %collective-permute-start) | collective-permute-done | bytes 262176 | tf_op jit(solution)/shard_map/while/body/eval_jaxpr/ppermute | solution.py:18
  149.4 3.3 %conditional.5 = ((f32[4,4,128]{2,1,0:T(4,128)}, f32[4,4,128]{2,1,0:T(4,128)S(1)}, f32[4,4,128,128]{3,2,1,0:T(8,128)S(1)})) conditional(s32[]{:T(128)} %convert_element_type.72, (f32[4,4,128]{2,1,0:T(4,128)}, f32[4,4,128]{2,1,0:T(4,128)S(1)}, f32[4,4,128,128]{3,2,1,0:T(8,128)S(1)}) %tuple.77, (pred[128,128]{0,1:T(8,128)(4,1)S(1)}, ...), branch_computations={%region_12.12_spmd, %region_13.15_spmd} | conditional | flops 137105408 | bytes 6733856 | solution.py:78
  156.9 6.4 %collective-permute-done = bf16[2,128,512]{1,2,0:T(8,128)(2,1)S(1)} collective-permute-done((bf16[2,128,512]{1,2,0:T(8,128)(2,1)}, bf16[2,128,512]{1,2,0:T(8,128)(2,1)S(1)}, u32[]{:S(2)}, u32[]{:S(2)}) %collective-permute-start) | collective-permute-done | bytes 262176 | tf_op jit(solution)/shard_map/while/body/eval_jaxpr/ppermute | solution.py:18
  163.3 3.3 %conditional.5 = ((f32[4,4,128]{2,1,0:T(4,128)}, f32[4,4,128]{2,1,0:T(4,128)S(1)}, f32[4,4,128,128]{3,2,1,0:T(8,128)S(1)})) conditional(s32[]{:T(128)} %convert_element_type.72, (f32[4,4,128]{2,1,0:T(4,128)}, f32[4,4,128]{2,1,0:T(4,128)S(1)}, f32[4,4,128,128]{3,2,1,0:T(8,128)S(1)}) %tuple.77, (pred[128,128]{0,1:T(8,128)(4,1)S(1)}, ...), branch_computations={%region_12.12_spmd, %region_13.15_spmd} | conditional | flops 137105408 | bytes 6733856 | solution.py:78
  170.9 6.4 %collective-permute-done = bf16[2,128,512]{1,2,0:T(8,128)(2,1)S(1)} collective-permute-done((bf16[2,128,512]{1,2,0:T(8,128)(2,1)}, bf16[2,128,512]{1,2,0:T(8,128)(2,1)S(1)}, u32[]{:S(2)}, u32[]{:S(2)}) %collective-permute-start) | collective-permute-done | bytes 262176 | tf_op jit(solution)/shard_map/while/body/eval_jaxpr/ppermute | solution.py:18
  177.3 3.3 %conditional.5 = ((f32[4,4,128]{2,1,0:T(4,128)}, f32[4,4,128]{2,1,0:T(4,128)S(1)}, f32[4,4,128,128]{3,2,1,0:T(8,128)S(1)})) conditional(s32[]{:T(128)} %convert_element_type.72, (f32[4,4,128]{2,1,0:T(4,128)}, f32[4,4,128]{2,1,0:T(4,128)S(1)}, f32[4,4,128,128]{3,2,1,0:T(8,128)S(1)}) %tuple.77, (pred[128,128]{0,1:T(8,128)(4,1)S(1)}, ...), branch_computations={%region_12.12_spmd, %region_13.15_spmd} | conditional | flops 137105408 | bytes 6733856 | solution.py:78
  184.9 6.4 %collective-permute-done = bf16[2,128,512]{1,2,0:T(8,128)(2,1)S(1)} collective-permute-done((bf16[2,128,512]{1,2,0:T(8,128)(2,1)}, bf16[2,128,512]{1,2,0:T(8,128)(2,1)S(1)}, u32[]{:S(2)}, u32[]{:S(2)}) %collective-permute-start) | collective-permute-done | bytes 262176 | tf_op jit(solution)/shard_map/while/body/eval_jaxpr/ppermute | solution.py:18
  191.3 3.3 %conditional.5 = ((f32[4,4,128]{2,1,0:T(4,128)}, f32[4,4,128]{2,1,0:T(4,128)S(1)}, f32[4,4,128,128]{3,2,1,0:T(8,128)S(1)})) conditional(s32[]{:T(128)} %convert_element_type.72, (f32[4,4,128]{2,1,0:T(4,128)}, f32[4,4,128]{2,1,0:T(4,128)S(1)}, f32[4,4,128,128]{3,2,1,0:T(8,128)S(1)}) %tuple.77, (pred[128,128]{0,1:T(8,128)(4,1)S(1)}, ...), branch_computations={%region_12.12_spmd, %region_13.15_spmd} | conditional | flops 137105408 | bytes 6733856 | solution.py:78
  198.9 6.4 %collective-permute-done = bf16[2,128,512]{1,2,0:T(8,128)(2,1)S(1)} collective-permute-done((bf16[2,128,512]{1,2,0:T(8,128)(2,1)}, bf16[2,128,512]{1,2,0:T(8,128)(2,1)S(1)}, u32[]{:S(2)}, u32[]{:S(2)}) %collective-permute-start) | collective-permute-done | bytes 262176 | tf_op jit(solution)/shard_map/while/body/eval_jaxpr/ppermute | solution.py:18
  205.3 3.3 %conditional.5 = ((f32[4,4,128]{2,1,0:T(4,128)}, f32[4,4,128]{2,1,0:T(4,128)S(1)}, f32[4,4,128,128]{3,2,1,0:T(8,128)S(1)})) conditional(s32[]{:T(128)} %convert_element_type.72, (f32[4,4,128]{2,1,0:T(4,128)}, f32[4,4,128]{2,1,0:T(4,128)S(1)}, f32[4,4,128,128]{3,2,1,0:T(8,128)S(1)}) %tuple.77, (pred[128,128]{0,1:T(8,128)(4,1)S(1)}, ...), branch_computations={%region_12.12_spmd, %region_13.15_spmd} | conditional | flops 137105408 | bytes 6733856 | solution.py:78
  212.9 6.4 %collective-permute-done = bf16[2,128,512]{1,2,0:T(8,128)(2,1)S(1)} collective-permute-done((bf16[2,128,512]{1,2,0:T(8,128)(2,1)}, bf16[2,128,512]{1,2,0:T(8,128)(2,1)S(1)}, u32[]{:S(2)}, u32[]{:S(2)}) %collective-permute-start) | collective-permute-done | bytes 262176 | tf_op jit(solution)/shard_map/while/body/eval_jaxpr/ppermute | solution.py:18
  219.3 3.3 %conditional.5 = ((f32[4,4,128]{2,1,0:T(4,128)}, f32[4,4,128]{2,1,0:T(4,128)S(1)}, f32[4,4,128,128]{3,2,1,0:T(8,128)S(1)})) conditional(s32[]{:T(128)} %convert_element_type.72, (f32[4,4,128]{2,1,0:T(4,128)}, f32[4,4,128]{2,1,0:T(4,128)S(1)}, f32[4,4,128,128]{3,2,1,0:T(8,128)S(1)}) %tuple.77, (pred[128,128]{0,1:T(8,128)(4,1)S(1)}, ...), branch_computations={%region_12.12_spmd, %region_13.15_spmd} | conditional | flops 137105408 | bytes 6733856 | solution.py:78
  226.9 6.4 %collective-permute-done = bf16[2,128,512]{1,2,0:T(8,128)(2,1)S(1)} collective-permute-done((bf16[2,128,512]{1,2,0:T(8,128)(2,1)}, bf16[2,128,512]{1,2,0:T(8,128)(2,1)S(1)}, u32[]{:S(2)}, u32[]{:S(2)}) %collective-permute-start) | collective-permute-done | bytes 262176 | tf_op jit(solution)/shard_map/while/body/eval_jaxpr/ppermute | solution.py:18
  233.3 3.3 %conditional.5 = ((f32[4,4,128]{2,1,0:T(4,128)}, f32[4,4,128]{2,1,0:T(4,128)S(1)}, f32[4,4,128,128]{3,2,1,0:T(8,128)S(1)})) conditional(s32[]{:T(128)} %convert_element_type.72, (f32[4,4,128]{2,1,0:T(4,128)}, f32[4,4,128]{2,1,0:T(4,128)S(1)}, f32[4,4,128,128]{3,2,1,0:T(8,128)S(1)}) %tuple.77, (pred[128,128]{0,1:T(8,128)(4,1)S(1)}, ...), branch_computations={%region_12.12_spmd, %region_13.15_spmd} | conditional | flops 137105408 | bytes 6733856 | solution.py:78
  (256 shorter events, 124.5 us)
Async XLA Ops:
  0.0 1.1 copy-start
  0.0 0.8 copy-start.6
  2.8 13.1 %copy-start.2 = (bf16[128,512]{1,0:T(8,128)(2,1)S(1)}, bf16[128,512]{1,0:T(8,128)(2,1)}, u32[]{:S(2)}) copy-start(bf16[128,512]{1,0:T(8,128)(2,1)} %param.13) | copy-start | bytes 393220
  2.8 19.0 %all-to-all-start = ((bf16[16,8,2048]{2,1,0:T(8,128)(2,1)}), bf16[16,8,2048]{2,1,0:T(8,128)(2,1)S(1)}, u32[]{:S(2)}, u32[]{:S(2)}) async-start(bf16[16,8,2048]{2,1,0:T(8,128)(2,1)} %copy.49), calls=%async_computation | async-start | bytes 1048576 | tf_op jit(solution)/shard_map/all_to_all | solution.py:139
  12.7 0.7 copy-start.7
  15.9 0.9 copy-start.1
  22.2 0.7 copy-start.3
  22.9 1.0 copy-start.4
  25.5 0.7 copy-start.5
  27.5 10.0 %collective-permute-start = (bf16[2,128,512]{1,2,0:T(8,128)(2,1)}, bf16[2,128,512]{1,2,0:T(8,128)(2,1)S(1)}, u32[]{:S(2)}, u32[]{:S(2)}) collective-permute-start(bf16[2,128,512]{1,2,0:T(8,128)(2,1)} %get-tuple-element.526), channel_id=1, source_target_pairs={{0,2},{2,4},{4,6},{6,8},{8,10},{10,12},{12,14},{14,16},{16,18},{18... | collective-permute-start | bytes 786440 | tf_op jit(solution)/shard_map/while/body/eval_jaxpr/ppermute | solution.py:18
  41.5 10.0 %collective-permute-start = (bf16[2,128,512]{1,2,0:T(8,128)(2,1)}, bf16[2,128,512]{1,2,0:T(8,128)(2,1)S(1)}, u32[]{:S(2)}, u32[]{:S(2)}) collective-permute-start(bf16[2,128,512]{1,2,0:T(8,128)(2,1)} %get-tuple-element.526), channel_id=1, source_target_pairs={{0,2},{2,4},{4,6},{6,8},{8,10},{10,12},{12,14},{14,16},{16,18},{18... | collective-permute-start | bytes 786440 | tf_op jit(solution)/shard_map/while/body/eval_jaxpr/ppermute | solution.py:18
  55.4 10.0 %collective-permute-start = (bf16[2,128,512]{1,2,0:T(8,128)(2,1)}, bf16[2,128,512]{1,2,0:T(8,128)(2,1)S(1)}, u32[]{:S(2)}, u32[]{:S(2)}) collective-permute-start(bf16[2,128,512]{1,2,0:T(8,128)(2,1)} %get-tuple-element.526), channel_id=1, source_target_pairs={{0,2},{2,4},{4,6},{6,8},{8,10},{10,12},{12,14},{14,16},{16,18},{18... | collective-permute-start | bytes 786440 | tf_op jit(solution)/shard_map/while/body/eval_jaxpr/ppermute | solution.py:18
  69.4 10.0 %collective-permute-start = (bf16[2,128,512]{1,2,0:T(8,128)(2,1)}, bf16[2,128,512]{1,2,0:T(8,128)(2,1)S(1)}, u32[]{:S(2)}, u32[]{:S(2)}) collective-permute-start(bf16[2,128,512]{1,2,0:T(8,128)(2,1)} %get-tuple-element.526), channel_id=1, source_target_pairs={{0,2},{2,4},{4,6},{6,8},{8,10},{10,12},{12,14},{14,16},{16,18},{18... | collective-permute-start | bytes 786440 | tf_op jit(solution)/shard_map/while/body/eval_jaxpr/ppermute | solution.py:18
  83.4 10.0 %collective-permute-start = (bf16[2,128,512]{1,2,0:T(8,128)(2,1)}, bf16[2,128,512]{1,2,0:T(8,128)(2,1)S(1)}, u32[]{:S(2)}, u32[]{:S(2)}) collective-permute-start(bf16[2,128,512]{1,2,0:T(8,128)(2,1)} %get-tuple-element.526), channel_id=1, source_target_pairs={{0,2},{2,4},{4,6},{6,8},{8,10},{10,12},{12,14},{14,16},{16,18},{18... | collective-permute-start | bytes 786440 | tf_op jit(solution)/shard_map/while/body/eval_jaxpr/ppermute | solution.py:18
  97.4 10.0 %collective-permute-start = (bf16[2,128,512]{1,2,0:T(8,128)(2,1)}, bf16[2,128,512]{1,2,0:T(8,128)(2,1)S(1)}, u32[]{:S(2)}, u32[]{:S(2)}) collective-permute-start(bf16[2,128,512]{1,2,0:T(8,128)(2,1)} %get-tuple-element.526), channel_id=1, source_target_pairs={{0,2},{2,4},{4,6},{6,8},{8,10},{10,12},{12,14},{14,16},{16,18},{18... | collective-permute-start | bytes 786440 | tf_op jit(solution)/shard_map/while/body/eval_jaxpr/ppermute | solution.py:18
  111.4 10.0 %collective-permute-start = (bf16[2,128,512]{1,2,0:T(8,128)(2,1)}, bf16[2,128,512]{1,2,0:T(8,128)(2,1)S(1)}, u32[]{:S(2)}, u32[]{:S(2)}) collective-permute-start(bf16[2,128,512]{1,2,0:T(8,128)(2,1)} %get-tuple-element.526), channel_id=1, source_target_pairs={{0,2},{2,4},{4,6},{6,8},{8,10},{10,12},{12,14},{14,16},{16,18},{18... | collective-permute-start | bytes 786440 | tf_op jit(solution)/shard_map/while/body/eval_jaxpr/ppermute | solution.py:18
  125.4 10.0 %collective-permute-start = (bf16[2,128,512]{1,2,0:T(8,128)(2,1)}, bf16[2,128,512]{1,2,0:T(8,128)(2,1)S(1)}, u32[]{:S(2)}, u32[]{:S(2)}) collective-permute-start(bf16[2,128,512]{1,2,0:T(8,128)(2,1)} %get-tuple-element.526), channel_id=1, source_target_pairs={{0,2},{2,4},{4,6},{6,8},{8,10},{10,12},{12,14},{14,16},{16,18},{18... | collective-permute-start | bytes 786440 | tf_op jit(solution)/shard_map/while/body/eval_jaxpr/ppermute | solution.py:18
  139.4 10.0 %collective-permute-start = (bf16[2,128,512]{1,2,0:T(8,128)(2,1)}, bf16[2,128,512]{1,2,0:T(8,128)(2,1)S(1)}, u32[]{:S(2)}, u32[]{:S(2)}) collective-permute-start(bf16[2,128,512]{1,2,0:T(8,128)(2,1)} %get-tuple-element.526), channel_id=1, source_target_pairs={{0,2},{2,4},{4,6},{6,8},{8,10},{10,12},{12,14},{14,16},{16,18},{18... | collective-permute-start | bytes 786440 | tf_op jit(solution)/shard_map/while/body/eval_jaxpr/ppermute | solution.py:18
  153.3 10.0 %collective-permute-start = (bf16[2,128,512]{1,2,0:T(8,128)(2,1)}, bf16[2,128,512]{1,2,0:T(8,128)(2,1)S(1)}, u32[]{:S(2)}, u32[]{:S(2)}) collective-permute-start(bf16[2,128,512]{1,2,0:T(8,128)(2,1)} %get-tuple-element.526), channel_id=1, source_target_pairs={{0,2},{2,4},{4,6},{6,8},{8,10},{10,12},{12,14},{14,16},{16,18},{18... | collective-permute-start | bytes 786440 | tf_op jit(solution)/shard_map/while/body/eval_jaxpr/ppermute | solution.py:18
  167.3 10.0 %collective-permute-start = (bf16[2,128,512]{1,2,0:T(8,128)(2,1)}, bf16[2,128,512]{1,2,0:T(8,128)(2,1)S(1)}, u32[]{:S(2)}, u32[]{:S(2)}) collective-permute-start(bf16[2,128,512]{1,2,0:T(8,128)(2,1)} %get-tuple-element.526), channel_id=1, source_target_pairs={{0,2},{2,4},{4,6},{6,8},{8,10},{10,12},{12,14},{14,16},{16,18},{18... | collective-permute-start | bytes 786440 | tf_op jit(solution)/shard_map/while/body/eval_jaxpr/ppermute | solution.py:18
  181.3 10.0 %collective-permute-start = (bf16[2,128,512]{1,2,0:T(8,128)(2,1)}, bf16[2,128,512]{1,2,0:T(8,128)(2,1)S(1)}, u32[]{:S(2)}, u32[]{:S(2)}) collective-permute-start(bf16[2,128,512]{1,2,0:T(8,128)(2,1)} %get-tuple-element.526), channel_id=1, source_target_pairs={{0,2},{2,4},{4,6},{6,8},{8,10},{10,12},{12,14},{14,16},{16,18},{18... | collective-permute-start | bytes 786440 | tf_op jit(solution)/shard_map/while/body/eval_jaxpr/ppermute | solution.py:18
  195.3 10.0 %collective-permute-start = (bf16[2,128,512]{1,2,0:T(8,128)(2,1)}, bf16[2,128,512]{1,2,0:T(8,128)(2,1)S(1)}, u32[]{:S(2)}, u32[]{:S(2)}) collective-permute-start(bf16[2,128,512]{1,2,0:T(8,128)(2,1)} %get-tuple-element.526), channel_id=1, source_target_pairs={{0,2},{2,4},{4,6},{6,8},{8,10},{10,12},{12,14},{14,16},{16,18},{18... | collective-permute-start | bytes 786440 | tf_op jit(solution)/shard_map/while/body/eval_jaxpr/ppermute | solution.py:18
  209.3 10.0 %collective-permute-start = (bf16[2,128,512]{1,2,0:T(8,128)(2,1)}, bf16[2,128,512]{1,2,0:T(8,128)(2,1)S(1)}, u32[]{:S(2)}, u32[]{:S(2)}) collective-permute-start(bf16[2,128,512]{1,2,0:T(8,128)(2,1)} %get-tuple-element.526), channel_id=1, source_target_pairs={{0,2},{2,4},{4,6},{6,8},{8,10},{10,12},{12,14},{14,16},{16,18},{18... | collective-permute-start | bytes 786440 | tf_op jit(solution)/shard_map/while/body/eval_jaxpr/ppermute | solution.py:18
  223.3 10.0 %collective-permute-start = (bf16[2,128,512]{1,2,0:T(8,128)(2,1)}, bf16[2,128,512]{1,2,0:T(8,128)(2,1)S(1)}, u32[]{:S(2)}, u32[]{:S(2)}) collective-permute-start(bf16[2,128,512]{1,2,0:T(8,128)(2,1)} %get-tuple-element.526), channel_id=1, source_target_pairs={{0,2},{2,4},{4,6},{6,8},{8,10},{10,12},{12,14},{14,16},{16,18},{18... | collective-permute-start | bytes 786440 | tf_op jit(solution)/shard_map/while/body/eval_jaxpr/ppermute | solution.py:18
where the time goes:
time: 242 us; the launch traced here: 239 us
  waiting for transfers between devices  100 us (41%)
  other arithmetic  43.1 us (18%)
  starting transfers between devices  38.1 us (16%)
  local copies, waits for them, and re-layouts  28.3 us (12%)
  matrix products  17.9 us (7%)
  loops' own time  10.8 us (4%)
    ppermute x15, waiting for transfers between devices, passed_along(): return lax.ppermute(value, axis, pairs)  96.1 us
    ppermute x15, starting transfers between devices, passed_along(): return lax.ppermute(value, axis, pairs)  28.7 us
    reduce_or x16, other arithmetic, absorb(): jnp.any(visible)  12.5 us
    add x16, other arithmetic, update(): totals = totals * shrink + jnp.sum(weights, axis=-1)  11.3 us
    dot_general x16, matrix products, update(): jnp.einsum('kgqt,tkd->kgqd', weights.astype(jnp.bfloat16), value_rows, pr...  11.2 us
    max x15, other arithmetic, update(): new_max = jnp.maximum(running_max, jnp.max(scores, axis=-1))  10.6 us
    another operation x1, loops' own time, circulate(): states, packed = lax.fori_loop(1, cycle_size, turn, (states, packed))  10.5 us
    while x15, local copies, waits for them, and re-layouts  10.4 us
  transfers between devices with their start and end apart: 16, of which 16 were waited for; matrix products, arithmetic and copies ran while one was open for 8% of the time, Pallas kernels for 0%

commit v1 on v0

v1 whole, which is shorter than its diff:
```python
import math

import jax
import jax.numpy as jnp
from jax import lax
from jax.experimental import pallas as pl
from jax.experimental.pallas import tpu as pltpu
from jax.sharding import PartitionSpec as P

HEAD = 128
CTX = 16
TOK = 128
BR = 8
NDOC = 16
GROUPS = 4
GROUP_HEADS = 4
PART = 32
REACH = 8
CHUNK = 384
MASKED = -1e30
SCALE = math.log2(math.e) / math.sqrt(HEAD)
ROWS_BY_ROWS = (((1,), (1,)), ((), ()))
ROWS_BY_COLS = (((1,), (0,)), ((), ()))


def dot(a, b, dims):
    return lax.dot_general(a, b, dims, preferred_element_type=jnp.float32)


def pack_kernel(owner_ref, q_ref, k_ref, v_ref, out_ref):
    me = lax.axis_index("ctx")
    lane = lax.broadcasted_iota(jnp.int32, (1, TOK), 1)
    goal = lane % BR
    for b in range(CTX):
        owner = owner_ref[me, b]
        rank = ((owner // 8) * 2 + owner % 2) * 4 + (owner // 2) % 4
        goal = goal + jnp.where(lane // BR == b, rank * BR, 0)
    row = lax.broadcasted_iota(jnp.int32, (TOK, TOK), 0)
    order = jnp.where(row == goal, 1.0, 0.0).astype(jnp.bfloat16)
    moved = dot(order, q_ref[...], ROWS_BY_COLS).astype(jnp.bfloat16)
    for g in range(GROUPS):
        cols = slice(g * HEAD, (g + 1) * HEAD)
        keys = k_ref[:, cols]
        vals = v_ref[:, cols].T
        for part in range(4):
            dest = (part // 2) * 8 + g * 2 + part % 2
            rows = slice(part * PART, (part + 1) * PART)
            for h in range(GROUP_HEADS):
                at = (g * GROUP_HEADS + h) * HEAD
                out_ref[dest, h * PART : (h + 1) * PART, :] = moved[rows, at : at + HEAD]
            out_ref[dest, 128:256, :] = keys
            out_ref[dest, 256:384, :] = vals


def attend_kernel(doc_ref, owner_ref, data_ref, out_ref, acc_ref):
    me = lax.axis_index("ctx")
    lane = lax.broadcasted_iota(jnp.int32, (CTX, TOK), 1)
    shard = lax.broadcasted_iota(jnp.int32, (CTX, TOK), 0)
    owner = (me // 8) * 8 + ((lane // BR) % 4) * 2 + me % 2
    owners = owner_ref[...]
    pos = shard * TOK + lane % BR
    for b in range(CTX):
        pos = pos + jnp.where(owners[:, b : b + 1] == owner, b * BR, 0)
    start = jnp.zeros((CTX, TOK), jnp.int32)
    end = jnp.int32(0)
    for n in range(NDOC - 1):
        end = end + doc_ref[n]
        start = jnp.where(pos >= end, end, start)
    key_at = lax.broadcasted_iota(jnp.int32, (TOK, TOK), 0)

    def scores(pair):
        shards = (2 * pair, 2 * pair + 1)
        tiles = range(max(0, shards[0] - REACH), shards[1] + 1)
        q = jnp.concatenate([data_ref[s, 0:128, :] for s in shards], 0)
        kept = ({}, {})
        peak = [None, None]
        for kb in tiles:
            both = dot(data_ref[kb, 128:256, :], q, ROWS_BY_ROWS)
            for i, s in enumerate(shards):
                if not s - REACH <= kb <= s:
                    continue
                one = both[:, i * TOK : (i + 1) * TOK]
                seen = key_at >= start[s : s + 1] - kb * TOK
                if kb == s:
                    seen = seen & (key_at <= pos[s : s + 1] - kb * TOK)
                one = jnp.where(seen, one, MASKED)
                kept[i][kb] = one
                top = jnp.max(one.reshape(16, 8, TOK), axis=0)
                peak[i] = top if peak[i] is None else jnp.maximum(peak[i], top)
        return shards, tiles, kept, peak

    def finish(state):
        shards, tiles, kept, peak = state
        weights, totals = [], []
        for i in range(2):
            top = jnp.max(peak[i], axis=0, keepdims=True) * SCALE
            total = jnp.zeros((8, TOK), jnp.float32)
            rounded = {}
            for kb, one in kept[i].items():
                w = jnp.exp2(one * SCALE - top)
                total = total + jnp.sum(w.reshape(16, 8, TOK), axis=0)
                rounded[kb] = w.astype(jnp.bfloat16)
            weights.append(rounded)
            totals.append(jnp.sum(total, axis=0, keepdims=True))
        none = jnp.zeros((TOK, TOK), jnp.bfloat16)
        wide = jnp.concatenate(
            [jnp.concatenate([weights[i].get(kb, none) for i in range(2)], 1) for kb in tiles], 0
        )
        vals = jnp.concatenate([data_ref[kb, 256:384, :] for kb in tiles], 1)
        mixed = dot(vals, wide, ROWS_BY_COLS)
        for i, s in enumerate(shards):
            rows = (mixed[:, i * TOK : (i + 1) * TOK] * (1.0 / totals[i])).T
            for h in range(GROUP_HEADS):
                for y in range(4):
                    at = h * PART + y * BR
                    acc_ref[y, s * BR : (s + 1) * BR, h * HEAD : (h + 1) * HEAD] = rows[at : at + BR]

    ahead = scores(0)
    for pair in range(1, CTX // 2):
        following = scores(pair)
        finish(ahead)
        ahead = following
    finish(ahead)
    out_ref[...] = acc_ref[...].astype(jnp.bfloat16)


SMEM = pl.BlockSpec(memory_space=pltpu.SMEM)
VMEM = pl.BlockSpec(memory_space=pltpu.VMEM)


def body(queries, keys, values, doc_lengths, owner_map):
    packed = pl.pallas_call(
        pack_kernel,
        out_shape=jax.ShapeDtypeStruct((CTX, CHUNK, HEAD), jnp.bfloat16),
        in_specs=[SMEM, VMEM, VMEM, VMEM],
        out_specs=VMEM,
        compiler_params=pltpu.CompilerParams(vmem_limit_bytes=24 << 20),
        name="pack",
    )(owner_map, queries, keys, values)
    data = lax.all_to_all(packed, "ctx", 0, 0, tiled=True)
    mixed = pl.pallas_call(
        attend_kernel,
        out_shape=jax.ShapeDtypeStruct((4, TOK, GROUP_HEADS * HEAD), jnp.bfloat16),
        in_specs=[SMEM, VMEM, VMEM],
        out_specs=VMEM,
        scratch_shapes=[pltpu.VMEM((4, TOK, GROUP_HEADS * HEAD), jnp.float32)],
        compiler_params=pltpu.CompilerParams(vmem_limit_bytes=40 << 20),
        name="attend",
    )(doc_lengths, owner_map, data)
    rings = [[x * 8 + y * 2 + c for y in range(4)] for x in range(2) for c in range(2)]
    back = lax.all_to_all(mixed, "ctx", 0, 0, tiled=True, axis_index_groups=rings)
    return back.transpose(1, 0, 2).reshape(TOK, GROUPS * GROUP_HEADS * HEAD)


def solution(mesh):
    placed = (
        P(("dp", "ctx"), "head"),
        P(("dp", "ctx"), "head"),
        P(("dp", "ctx"), "head"),
        P("dp"),
        P("dp", None),
    )
    return jax.shard_map(
        body, mesh=mesh, in_specs=placed, out_specs=P(("dp", "ctx"), "head"), check_vma=False
    )
```

time: 242 us -> 52.1 us (0.22)
  the two profiles are of different devices: /device:TPU:2 before, /device:TPU:1 now
where the time goes in v1:
time: 52.1 us; the launch traced here: 51.8 us
  blocking collectives  41.7 us (80%)
  Pallas kernels  5.14 us (10%)
  local copies, waits for them, and re-layouts  4.84 us (9%)
    all_to_all x1, blocking collectives, body(): data = lax.all_to_all(packed, 'ctx', 0, 0, tiled=True)  30.4 us
    all_to_all x1, blocking collectives, body(): lax.all_to_all(mixed, 'ctx', 0, 0, tiled=True, axis_index_groups=rings)  11.3 us
    pallas_call x1, Pallas kernels, body(): pl.pallas_call(attend_kernel, out_shape=jax.ShapeDtypeStruct((4, TOK, GRO...  3.96 us
    unnamed x12, local copies, waits for them, and re-layouts  3.56 us
    pallas_call x1, Pallas kernels, body(): pl.pallas_call(pack_kernel, out_shape=jax.ShapeDtypeStruct((CTX, CHUNK, H...  1.18 us

profile of v1, /device:TPU:1, one launch (start us, length us, event | category | flops | bytes accessed | tf_op | source)
XLA Modules:
  0.0 51.8 jit_solution(3503171093234816578)
XLA Ops:
  0.0 0.0 copy-start
  0.0 1.0 %copy-done = bf16[128,2048]{1,0:T(8,128)(2,1)S(1)} copy-done((bf16[128,2048]{1,0:T(8,128)(2,1)S(1)}, bf16[128,2048]{1,0:T(8,128)(2,1)}, u32[]{:S(2)}) %copy-start) | copy-done | bytes 524312
  1.0 0.0 copy-start.1
  1.0 0.9 %copy-done.1 = bf16[128,512]{1,0:T(8,128)(2,1)S(1)} copy-done((bf16[128,512]{1,0:T(8,128)(2,1)S(1)}, bf16[128,512]{1,0:T(8,128)(2,1)}, u32[]{:S(2)}) %copy-start.1) | copy-done | bytes 131096
  1.9 0.0 copy-start.2
  1.9 0.9 %copy-done.2 = bf16[128,512]{1,0:T(8,128)(2,1)S(1)} copy-done((bf16[128,512]{1,0:T(8,128)(2,1)S(1)}, bf16[128,512]{1,0:T(8,128)(2,1)}, u32[]{:S(2)}) %copy-start.2) | copy-done | bytes 131096
  2.9 0.0 copy-start.3
  2.9 0.7 %copy-done.3 = s32[16,16]{1,0:T(8,128)S(1)} copy-done((s32[16,16]{1,0:T(8,128)S(1)}, s32[16,16]{1,0:T(8,128)}, u32[]{:S(2)}) %copy-start.3) | copy-done | bytes 1048
  3.5 1.2 %pack.1 = bf16[16,384,128]{2,1,0:T(8,128)(2,1)S(1)} custom-call(s32[16,16]{1,0:T(8,128)S(1)} %copy-done.3, bf16[128,2048]{1,0:T(8,128)(2,1)S(1)} %copy-done, bf16[128,512]{1,0:T(8,128)(2,1)S(1)} %copy-done.1, bf16[128,512]{1,0:T(8,128)(2,1)S(1)} %copy-done.2), custom_call_target="tpu_custom_call" | custom-call | tf_op jit(solution)/shard_map/pack/pallas_call | solution.py:132
  4.7 0.0 copy-start.4
  4.8 0.0 copy-start.5
  4.8 30.4 %all_to_all.10.data_ref = bf16[16,384,128]{2,1,0:T(8,128)(2,1)S(1)} all-to-all(bf16[16,384,128]{2,1,0:T(8,128)(2,1)S(1)} %pack.1), channel_id=1, replica_groups=mesh['dp'=16,'ctx'=16,'head'=2] {'ctx'}, dimensions={0} | all-to-all | bytes 3145728 | tf_op jit(solution)/shard_map/all_to_all | solution.py:140
  35.2 0.0 copy-done.4
  35.2 0.0 copy-done.5
  35.2 4.0 %attend.1 = bf16[4,128,512]{2,1,0:T(8,128)(2,1)S(1)} custom-call(s32[16]{0:T(128)S(1)} %copy-done.5, s32[16,16]{1,0:T(8,128)S(1)} %copy-done.4, bf16[16,384,128]{2,1,0:T(8,128)(2,1)S(1)} %all_to_all.10.data_ref), custom_call_target="tpu_custom_call" | custom-call | tf_op jit(solution)/shard_map/attend/pallas_call | solution.py:141
  39.2 11.3 %all_to_all.11 = bf16[4,128,512]{2,1,0:T(8,128)(2,1)S(1)} all-to-all(bf16[4,128,512]{2,1,0:T(8,128)(2,1)S(1)} %attend.1), channel_id=1, replica_groups={{0,4,8,12},{2,6,10,14},{16,20,24,28},{18,22,26,30},{1,5,9,13},{3,7,11,1..., dimensions={0} | all-to-all | bytes 1048576 | tf_op jit(solution)/shard_map/all_to_all | solution.py:151
  50.5 0.3 copy.6
  50.8 1.0 %copy.7 = bf16[128,2048]{1,0:T(8,128)(2,1)} copy(bf16[128,2048]{0,1:T(8,128)(2,1)S(1)} %bitcast.3) | data formatting | bytes 1048576 | tf_op jit(solution)/shard_map/reshape | solution.py:152
Async XLA Ops:
  0.0 1.0 %copy-start = (bf16[128,2048]{1,0:T(8,128)(2,1)S(1)}, bf16[128,2048]{1,0:T(8,128)(2,1)}, u32[]{:S(2)}) copy-start(bf16[128,2048]{1,0:T(8,128)(2,1)} %q_ref.1) | copy-start | bytes 1572868
  1.0 0.9 %copy-start.1 = (bf16[128,512]{1,0:T(8,128)(2,1)S(1)}, bf16[128,512]{1,0:T(8,128)(2,1)}, u32[]{:S(2)}) copy-start(bf16[128,512]{1,0:T(8,128)(2,1)} %k_ref.1) | copy-start | bytes 393220
  1.9 0.9 %copy-start.2 = (bf16[128,512]{1,0:T(8,128)(2,1)S(1)}, bf16[128,512]{1,0:T(8,128)(2,1)}, u32[]{:S(2)}) copy-start(bf16[128,512]{1,0:T(8,128)(2,1)} %v_ref.1) | copy-start | bytes 393220
  2.9 0.7 %copy-start.3 = (s32[16,16]{1,0:T(8,128)S(1)}, s32[16,16]{1,0:T(8,128)}, u32[]{:S(2)}) copy-start(s32[16,16]{1,0:T(8,128)} %owner_ref.3) | copy-start | bytes 3076
  4.7 30.5 %copy-start.4 = (s32[16,16]{1,0:T(8,128)S(1)}, s32[16,16]{1,0:T(8,128)}, u32[]{:S(2)}) copy-start(s32[16,16]{1,0:T(8,128)} %owner_ref.3) | copy-start | bytes 3076
  4.8 30.5 %copy-start.5 = (s32[16]{0:T(128)S(1)}, s32[16]{0:T(128)}, u32[]{:S(2)}) copy-start(s32[16]{0:T(128)} %doc_ref.1) | copy-start | bytes 196

commit v2 on v1

v2 whole, which is shorter than its diff:
```python
import math

import jax
import jax.numpy as jnp
from jax import lax
from jax.experimental import pallas as pl
from jax.experimental.pallas import tpu as pltpu
from jax.sharding import PartitionSpec as P

HEAD = 128
CTX = 16
TOK = 128
BR = 8
NDOC = 16
GROUPS = 4
GROUP_HEADS = 4
PART = 32
REACH = 8
CHUNK = 256
MASKED = -1e30
SCALE = math.log2(math.e) / math.sqrt(HEAD)
ROWS_BY_ROWS = (((1,), (1,)), ((), ()))
ROWS_BY_COLS = (((1,), (0,)), ((), ()))


def dot(a, b, dims):
    return lax.dot_general(a, b, dims, preferred_element_type=jnp.float32)


def pack_kernel(owner_any, doc_any, q_any, k_any, v_any, out_ref, rows_ref, owner_ref, owners_ref, doc_ref, q_ref, k_ref, v_ref, sems):
    me = lax.axis_index("ctx")
    moves = (
        (owner_any, owner_ref),
        (owner_any, owners_ref),
        (doc_any, doc_ref),
        (k_any, k_ref),
        (v_any, v_ref),
        (q_any, q_ref),
    )
    copies = [pltpu.make_async_copy(src, dst, sems.at[i]) for i, (src, dst) in enumerate(moves)]
    for copy in copies:
        copy.start()
    for copy in copies[:3]:
        copy.wait()
    one_lane = lax.broadcasted_iota(jnp.int32, (1, TOK), 1)
    goal = one_lane % BR
    for b in range(CTX):
        owner = owner_ref[me, b]
        rank = ((owner // 8) * 2 + owner % 2) * 4 + (owner // 2) % 4
        goal = goal + jnp.where(one_lane // BR == b, rank * BR, 0)
    row = lax.broadcasted_iota(jnp.int32, (TOK, TOK), 0)
    order = jnp.where(row == goal, 1.0, 0.0).astype(jnp.bfloat16)

    lane = lax.broadcasted_iota(jnp.int32, (CTX, TOK), 1)
    shard = lax.broadcasted_iota(jnp.int32, (CTX, TOK), 0)
    mine = (me // 8) * 8 + ((lane // BR) % 4) * 2 + me % 2
    owners = owners_ref[...]
    pos = shard * TOK + lane % BR
    for b in range(CTX):
        pos = pos + jnp.where(owners[:, b : b + 1] == mine, b * BR, 0)
    start = jnp.zeros((CTX, TOK), jnp.int32)
    end = jnp.int32(0)
    for n in range(NDOC - 1):
        end = end + doc_ref[n]
        start = jnp.where(pos >= end, end, start)
    rows_ref[0] = pos
    rows_ref[1] = start

    for copy in copies[3:5]:
        copy.wait()
    for g in range(GROUPS):
        cols = slice(g * HEAD, (g + 1) * HEAD)
        keys = k_ref[:, cols]
        vals = v_ref[:, cols].T
        for part in range(4):
            dest = (part // 2) * 8 + g * 2 + part % 2
            out_ref[dest, 128:256, :] = vals if part % 2 else keys
    copies[5].wait()
    for g in range(GROUPS):
        wide = slice(g * GROUP_HEADS * HEAD, (g + 1) * GROUP_HEADS * HEAD)
        moved = dot(order, q_ref[:, wide], ROWS_BY_COLS).astype(jnp.bfloat16)
        for part in range(4):
            dest = (part // 2) * 8 + g * 2 + part % 2
            for h in range(GROUP_HEADS):
                out_ref[dest, h * PART : (h + 1) * PART, :] = moved[
                    part * PART : (part + 1) * PART, h * HEAD : (h + 1) * HEAD
                ]


def attend_kernel(rows_ref, data_ref, both_ref, out_ref, acc_ref):
    key_at = lax.broadcasted_iota(jnp.int32, (TOK, TOK), 0)

    def scores(pair):
        shards = (2 * pair, 2 * pair + 1)
        tiles = range(max(0, shards[0] - REACH), shards[1] + 1)
        q = jnp.concatenate([data_ref[s, 0:128, :] for s in shards], 0)
        kept = ({}, {})
        peak = [None, None]
        for kb in tiles:
            both = dot(both_ref[0, kb], q, ROWS_BY_ROWS)
            for i, s in enumerate(shards):
                if not s - REACH <= kb <= s:
                    continue
                one = both[:, i * TOK : (i + 1) * TOK]
                seen = key_at >= rows_ref[1, s : s + 1, :] - kb * TOK
                if kb == s:
                    seen = seen & (key_at <= rows_ref[0, s : s + 1, :] - kb * TOK)
                one = jnp.where(seen, one, MASKED)
                kept[i][kb] = one
                top = jnp.max(one.reshape(16, 8, TOK), axis=0)
                peak[i] = top if peak[i] is None else jnp.maximum(peak[i], top)
        return shards, tiles, kept, peak

    def finish(state):
        shards, tiles, kept, peak = state
        weights, totals = [], []
        for i in range(2):
            top = jnp.max(peak[i], axis=0, keepdims=True) * SCALE
            total = jnp.zeros((8, TOK), jnp.float32)
            rounded = {}
            for kb, one in kept[i].items():
                w = jnp.exp2(one * SCALE - top)
                total = total + jnp.sum(w.reshape(16, 8, TOK), axis=0)
                rounded[kb] = w.astype(jnp.bfloat16)
            weights.append(rounded)
            totals.append(jnp.sum(total, axis=0, keepdims=True))
        none = jnp.zeros((TOK, TOK), jnp.bfloat16)
        wide = jnp.concatenate(
            [jnp.concatenate([weights[i].get(kb, none) for i in range(2)], 1) for kb in tiles], 0
        )
        vals = jnp.concatenate([both_ref[1, kb] for kb in tiles], 1)
        mixed = dot(vals, wide, ROWS_BY_COLS)
        for i, s in enumerate(shards):
            rows = (mixed[:, i * TOK : (i + 1) * TOK] * (1.0 / totals[i])).T
            for h in range(GROUP_HEADS):
                for y in range(4):
                    at = h * PART + y * BR
                    acc_ref[y, s * BR : (s + 1) * BR, h * HEAD : (h + 1) * HEAD] = rows[at : at + BR]

    ahead = scores(0)
    for pair in range(1, CTX // 2):
        following = scores(pair)
        finish(ahead)
        ahead = following
    finish(ahead)
    out_ref[...] = acc_ref[...].astype(jnp.bfloat16)


def unpack_kernel(in_ref, out_any, sems):
    wide = GROUP_HEADS * HEAD
    copies = [
        pltpu.make_async_copy(in_ref.at[g], out_any.at[:, g * wide : (g + 1) * wide], sems.at[g])
        for g in range(GROUPS)
    ]
    for copy in copies:
        copy.start()
    for copy in copies:
        copy.wait()


VMEM = pl.BlockSpec(memory_space=pltpu.VMEM)
ANY = pl.BlockSpec(memory_space=pl.ANY)


def body(queries, keys, values, doc_lengths, owner_map):
    packed, rows = pl.pallas_call(
        pack_kernel,
        out_shape=(
            jax.ShapeDtypeStruct((CTX, CHUNK, HEAD), jnp.bfloat16),
            jax.ShapeDtypeStruct((2, CTX, TOK), jnp.int32),
        ),
        in_specs=[ANY] * 5,
        out_specs=(VMEM, VMEM),
        scratch_shapes=[
            pltpu.SMEM((CTX, CTX), jnp.int32),
            pltpu.VMEM((CTX, CTX), jnp.int32),
            pltpu.SMEM((NDOC,), jnp.int32),
            pltpu.VMEM(queries.shape, jnp.bfloat16),
            pltpu.VMEM(keys.shape, jnp.bfloat16),
            pltpu.VMEM(values.shape, jnp.bfloat16),
            pltpu.SemaphoreType.DMA((6,)),
        ],
        compiler_params=pltpu.CompilerParams(vmem_limit_bytes=60 << 20),
        name="pack",
    )(owner_map, doc_lengths, queries, keys, values)
    data = lax.all_to_all(packed, "ctx", 0, 0, tiled=True)
    chips = [[2 * i, 2 * i + 1] for i in range(CTX // 2)]
    both = lax.all_gather(data[:, TOK:], "ctx", axis=0, axis_index_groups=chips)
    mixed = pl.pallas_call(
        attend_kernel,
        out_shape=jax.ShapeDtypeStruct((4, TOK, GROUP_HEADS * HEAD), jnp.bfloat16),
        in_specs=[VMEM, VMEM, VMEM],
        out_specs=VMEM,
        scratch_shapes=[pltpu.VMEM((4, TOK, GROUP_HEADS * HEAD), jnp.float32)],
        compiler_params=pltpu.CompilerParams(vmem_limit_bytes=40 << 20),
        name="attend",
    )(rows, data, both)
    rings = [[x * 8 + y * 2 + c for y in range(4)] for x in range(2) for c in range(2)]
    back = lax.all_to_all(mixed, "ctx", 0, 0, tiled=True, axis_index_groups=rings)
    return pl.pallas_call(
        unpack_kernel,
        out_shape=jax.ShapeDtypeStruct(queries.shape, jnp.bfloat16),
        in_specs=[VMEM],
        out_specs=ANY,
        scratch_shapes=[pltpu.SemaphoreType.DMA((GROUPS,))],
        compiler_params=pltpu.CompilerParams(vmem_limit_bytes=16 << 20),
        name="unpack",
    )(back)


def solution(mesh):
    placed = (
        P(("dp", "ctx"), "head"),
        P(("dp", "ctx"), "head"),
        P(("dp", "ctx"), "head"),
        P("dp"),
        P("dp", None),
    )
    return jax.shard_map(
        body, mesh=mesh, in_specs=placed, out_specs=P(("dp", "ctx"), "head"), check_vma=False
    )
```

time: 52.1 us -> 80.3 us (1.54)
  waiting for transfers between devices: 0 us -> 20.1 us
  between operations: 0.04 us -> 13.4 us
  blocking collectives: 41.7 us -> 37.7 us
  local copies, waits for them, and re-layouts: 4.84 us -> 2.06 us
  Pallas kernels: 5.14 us -> 6.71 us
    all_gather x0 -> x1, waiting for transfers between devices: none -> 20.1 us  [body(): both = lax.all_gather(data[:, TOK:], 'ctx', axis=0, axis_index_groups=chips)]
    all_to_all x1, blocking collectives: 30.4 us -> 25.8 us  [body(): data = lax.all_to_all(packed, 'ctx', 0, 0, tiled=True)]
    unnamed x12 -> x4, local copies, waits for them, and re-layouts: 3.56 us -> 1.23 us
    pallas_call x1 -> x2, Pallas kernels: 1.18 us -> 3.4 us  [the longest x1 2.58 us: body(): pl.pallas_call(pack_kernel, out_shape=(jax.ShapeDtypeStruct((CTX, CHUNK,...]
    reshape x1 -> x0, local copies, waits for them, and re-layouts: 1.01 us -> none  [body(): return back.transpose(1, 0, 2).reshape(TOK, GROUPS * GROUP_HEADS * HEAD)]
    slice x0 -> x1, local copies, waits for them, and re-layouts: none -> 0.83 us  [body(): both = lax.all_gather(data[:, TOK:], 'ctx', axis=0, axis_index_groups=chips)]
  transfers between devices with their start and end apart: 0 -> 1, of which waited for: 0 -> 1; matrix products, arithmetic and copies ran while one was open for 0% -> 0% of each run, Pallas kernels for 0% -> 0%
where the time goes in v2:
time: 80.3 us; the launch traced here: 80 us
  blocking collectives  37.7 us (47%)
  waiting for transfers between devices  20.1 us (25%)
  between operations  13.4 us (17%)
  Pallas kernels  6.71 us (8%)
  local copies, waits for them, and re-layouts  2.06 us (3%)
    all_to_all x1, blocking collectives, body(): data = lax.all_to_all(packed, 'ctx', 0, 0, tiled=True)  25.8 us
    all_gather x1, waiting for transfers between devices, body(): both = lax.all_gather(data[:, TOK:], 'ctx', axis=0, axis_index_groups=chips)  20.1 us
    all_to_all x1, blocking collectives, body(): lax.all_to_all(mixed, 'ctx', 0, 0, tiled=True, axis_index_groups=rings)  11.9 us
    pallas_call x1, Pallas kernels, body(): pl.pallas_call(attend_kernel, out_shape=jax.ShapeDtypeStruct((4, TOK, GRO...  3.31 us
    pallas_call x1, Pallas kernels, body(): pl.pallas_call(pack_kernel, out_shape=(jax.ShapeDtypeStruct((CTX, CHUNK,...  2.58 us
  transfers between devices with their start and end apart: 1, of which 1 were waited for; matrix products, arithmetic and copies ran while one was open for 0% of the time, Pallas kernels for 0%

profile of v2, /device:TPU:1, one launch (start us, length us, event | category | flops | bytes accessed | tf_op | source)
XLA Modules:
  0.0 80.0 jit_solution(10153765094912361114)
XLA Ops:
  6.5 0.0 all-gather.3.cloned.1.call-start
  6.5 2.6 %pack.1 = (bf16[16,256,128]{2,1,0:T(8,128)(2,1)}, s32[2,16,128]{2,1,0:T(8,128)}) custom-call(s32[16,16]{1,0:T(8,128)} %owner_any.1, s32[16]{0:T(128)} %doc_any.1, bf16[128,2048]{1,0:T(8,128)(2,1)} %q_any.1, bf16[128,512]{1,0:T(8,128)(2,1)} %k_any.1, bf16[128,512]{1,0:T(8,128)(2,1)} %v_any.1), custom_call_target="tpu_custom_call" | custom-call | tf_op jit(solution)/shard_map/pack/pallas_call | solution.py:166
  9.1 25.8 %all_to_all.10.data_ref = bf16[16,256,128]{2,1,0:T(8,128)(2,1)S(1)} all-to-all(bf16[16,256,128]{2,1,0:T(8,128)(2,1)} %get-tuple-element.8), channel_id=1, replica_groups=mesh['dp'=16,'ctx'=16,'head'=2] {'ctx'}, dimensions={0} | all-to-all | bytes 2097152 | tf_op jit(solution)/shard_map/all_to_all | solution.py:186
  34.9 0.8 %slice.4 = bf16[16,128,128]{2,1,0:T(8,128)(2,1)} slice(bf16[16,256,128]{2,1,0:T(8,128)(2,1)S(1)} %all_to_all.10.data_ref), slice={[0:16], [128:256], [0:128]} | slice | bytes 1048576 | tf_op jit(solution)/shard_map/slice | solution.py:188
  35.8 0.0 copy-start.1
  35.8 0.0 all-gather.3.cloned.1.call-update
  35.8 20.1 %all-gather.3.cloned.1.call-done = bf16[32,128,128]{2,1,0:T(8,128)(2,1)} async-done(((bf16[16,128,128]{2,1,0:T(8,128)(2,1)}), bf16[32,128,128]{2,1,0:T(8,128)(2,1)}) %all-gather.3.cloned.1.call-update) | async-done | bytes 1048592 | tf_op jit(solution)/shard_map/all_gather | solution.py:188
  55.9 0.0 copy-done.1
  55.9 0.0 copy-start
  55.9 1.2 %copy-done = bf16[32,128,128]{2,1,0:T(8,128)(2,1)S(1)} copy-done((bf16[32,128,128]{2,1,0:T(8,128)(2,1)S(1)}, bf16[32,128,128]{2,1,0:T(8,128)(2,1)}, u32[]{:S(2)}) %copy-start) | copy-done | bytes 1048600
  57.1 3.3 %attend.1 = bf16[4,128,512]{2,1,0:T(8,128)(2,1)S(1)} custom-call(s32[2,16,128]{2,1,0:T(8,128)S(1)} %copy-done.1, bf16[16,256,128]{2,1,0:T(8,128)(2,1)S(1)} %all_to_all.10.data_ref, bf16[2,16,128,128]{3,2,1,0:T(8,128)(2,1)S(1)} %bitcast.1), custom_call_target="tpu_custom_call" | custom-call | tf_op jit(solution)/shard_map/attend/pallas_call | solution.py:189
  60.4 11.9 %all_to_all.11.in_ref = bf16[4,128,512]{2,1,0:T(8,128)(2,1)S(1)} all-to-all(bf16[4,128,512]{2,1,0:T(8,128)(2,1)S(1)} %attend.1), channel_id=1, replica_groups={{0,4,8,12},{2,6,10,14},{16,20,24,28},{18,22,26,30},{1,5,9,13},{3,7,11,1..., dimensions={0} | all-to-all | bytes 1048576 | tf_op jit(solution)/shard_map/all_to_all | solution.py:199
  72.3 0.8 %unpack.1 = bf16[128,2048]{1,0:T(8,128)(2,1)} custom-call(bf16[4,128,512]{2,1,0:T(8,128)(2,1)S(1)} %all_to_all.11.in_ref), custom_call_target="tpu_custom_call" | custom-call | tf_op jit(solution)/shard_map/unpack/pallas_call | solution.py:200
Async XLA Ops:
  6.5 49.3 %all-gather.3.cloned.1.call-start = ((), (), s32[]{:S(2)}) async-start(), calls=%async_computation.2 | async-start | bytes 1572864 | tf_op jit(solution)/shard_map/all_gather | solution.py:188
  35.8 20.1 %copy-start.1 = (s32[2,16,128]{2,1,0:T(8,128)S(1)}, s32[2,16,128]{2,1,0:T(8,128)}, u32[]{:S(2)}) copy-start(s32[2,16,128]{2,1,0:T(8,128)} %get-tuple-element.7.rows_ref) | copy-start | bytes 49156
  55.9 1.2 %copy-start = (bf16[32,128,128]{2,1,0:T(8,128)(2,1)S(1)}, bf16[32,128,128]{2,1,0:T(8,128)(2,1)}, u32[]{:S(2)}) copy-start(bf16[32,128,128]{2,1,0:T(8,128)(2,1)} %all-gather.3.cloned.1.call-done) | copy-start | bytes 3145732
Sparse Core Ops, SparseCore 0:
  35.9 19.9 all-gather.2

commit v3 on v2

--- a/solution.py
+++ b/solution.py
@@ -87,7 +87,12 @@
                 ]
 
 
-def attend_kernel(rows_ref, data_ref, both_ref, out_ref, acc_ref):
+def attend_kernel(rows_ref, data_ref, other_ref, out_ref, acc_ref, both_ref):
+    first = lax.axis_index("ctx") % 2 == 0
+    for s in range(CTX):
+        own, far = data_ref[s, TOK:, :], other_ref[s]
+        both_ref[0, s] = jnp.where(first, own, far)
+        both_ref[1, s] = jnp.where(first, far, own)
     key_at = lax.broadcasted_iota(jnp.int32, (TOK, TOK), 0)
 
     def scores(pair):
@@ -184,17 +189,19 @@
         name="pack",
     )(owner_map, doc_lengths, queries, keys, values)
     data = lax.all_to_all(packed, "ctx", 0, 0, tiled=True)
-    chips = [[2 * i, 2 * i + 1] for i in range(CTX // 2)]
-    both = lax.all_gather(data[:, TOK:], "ctx", axis=0, axis_index_groups=chips)
+    other = lax.ppermute(data[:, TOK:], "ctx", [(i, i ^ 1) for i in range(CTX)])
     mixed = pl.pallas_call(
         attend_kernel,
         out_shape=jax.ShapeDtypeStruct((4, TOK, GROUP_HEADS * HEAD), jnp.bfloat16),
         in_specs=[VMEM, VMEM, VMEM],
         out_specs=VMEM,
-        scratch_shapes=[pltpu.VMEM((4, TOK, GROUP_HEADS * HEAD), jnp.float32)],
+        scratch_shapes=[
+            pltpu.VMEM((4, TOK, GROUP_HEADS * HEAD), jnp.float32),
+            pltpu.VMEM((2, CTX, TOK, HEAD), jnp.bfloat16),
+        ],
         compiler_params=pltpu.CompilerParams(vmem_limit_bytes=40 << 20),
         name="attend",
-    )(rows, data, both)
+    )(rows, data, other)
     rings = [[x * 8 + y * 2 + c for y in range(4)] for x in range(2) for c in range(2)]
     back = lax.all_to_all(mixed, "ctx", 0, 0, tiled=True, axis_index_groups=rings)
     return pl.pallas_call(

time: 80.3 us -> 49.2 us (0.61)
  waiting for transfers between devices: 20.1 us -> 1.51 us
  between operations: 13.4 us -> 0.03 us
  starting transfers between devices: 0.01 us -> 3.07 us
  local copies, waits for them, and re-layouts: 2.06 us -> 0.04 us
    all_gather x1 -> x0, waiting for transfers between devices: 20.1 us -> none  [body(): both = lax.all_gather(data[:, TOK:], 'ctx', axis=0, axis_index_groups=chips)]
    ppermute x0 -> x1, starting transfers between devices: none -> 3.07 us  [body(): other = lax.ppermute(data[:, TOK:], 'ctx', [(i, i ^ 1) for i in range(CTX)])]
    ppermute x0 -> x1, waiting for transfers between devices: none -> 1.51 us  [body(): other = lax.ppermute(data[:, TOK:], 'ctx', [(i, i ^ 1) for i in range(CTX)])]
    unnamed x4 -> x2, local copies, waits for them, and re-layouts: 1.23 us -> 0.01 us
where the time goes in v3:
time: 49.2 us; the launch traced here: 49 us
  blocking collectives  37.4 us (76%)
  Pallas kernels  6.85 us (14%)
  starting transfers between devices  3.07 us (6%)
  waiting for transfers between devices  1.51 us (3%)
    all_to_all x1, blocking collectives, body(): data = lax.all_to_all(packed, 'ctx', 0, 0, tiled=True)  25.8 us
    all_to_all x1, blocking collectives, body(): lax.all_to_all(mixed, 'ctx', 0, 0, tiled=True, axis_index_groups=rings)  11.6 us
    pallas_call x1, Pallas kernels, body(): pl.pallas_call(attend_kernel, out_shape=jax.ShapeDtypeStruct((4, TOK, GRO...  3.46 us
    ppermute x1, starting transfers between devices, body(): other = lax.ppermute(data[:, TOK:], 'ctx', [(i, i ^ 1) for i in range(CTX)])  3.07 us
    pallas_call x1, Pallas kernels, body(): pl.pallas_call(pack_kernel, out_shape=(jax.ShapeDtypeStruct((CTX, CHUNK,...  2.58 us
    ppermute x1, waiting for transfers between devices, body(): other = lax.ppermute(data[:, TOK:], 'ctx', [(i, i ^ 1) for i in range(CTX)])  1.51 us
  transfers between devices with their start and end apart: 1, of which 1 were waited for; matrix products, arithmetic and copies ran while one was open for 0% of the time, Pallas kernels for 0%

profile of v3, /device:TPU:1, one launch (start us, length us, event | category | flops | bytes accessed | tf_op | source)
XLA Modules:
  0.0 49.0 jit_solution(4552478926491274821)
XLA Ops:
  0.0 2.6 %pack.1 = (bf16[16,256,128]{2,1,0:T(8,128)(2,1)}, s32[2,16,128]{2,1,0:T(8,128)}) custom-call(s32[16,16]{1,0:T(8,128)} %owner_any.1, s32[16]{0:T(128)} %doc_any.1, bf16[128,2048]{1,0:T(8,128)(2,1)} %q_any.1, bf16[128,512]{1,0:T(8,128)(2,1)} %k_any.1, bf16[128,512]{1,0:T(8,128)(2,1)} %v_any.1), custom_call_target="tpu_custom_call" | custom-call | tf_op jit(solution)/shard_map/pack/pallas_call | solution.py:171
  2.6 25.8 %all_to_all.10.data_ref = bf16[16,256,128]{2,1,0:T(8,128)(2,1)S(1)} all-to-all(bf16[16,256,128]{2,1,0:T(8,128)(2,1)} %get-tuple-element.8), channel_id=1, replica_groups=mesh['dp'=16,'ctx'=16,'head'=2] {'ctx'}, dimensions={0} | all-to-all | bytes 2097152 | tf_op jit(solution)/shard_map/all_to_all | solution.py:191
  28.4 0.0 copy-start
  28.5 3.1 %collective-permute-start = (bf16[16,128,128]{2,1,0:T(8,128)(2,1)S(1)}, bf16[16,128,128]{2,1,0:T(8,128)(2,1)S(1)}, u32[]{:S(2)}, u32[]{:S(2)}) collective-permute-start(bf16[16,128,128]{2,1,0:T(8,128)(2,1)S(1)} %slice.4), channel_id=1, source_target_pairs={{0,2},{2,0},{4,6},{6,4},{8,10},{10,8},{12,14},{14,12},{16,18},{18,... | collective-permute-start | bytes 1572872 | tf_op jit(solution)/shard_map/ppermute | solution.py:192
  31.5 1.5 %collective-permute-done.other_ref = bf16[16,128,128]{2,1,0:T(8,128)(2,1)S(1)} collective-permute-done((bf16[16,128,128]{2,1,0:T(8,128)(2,1)S(1)}, bf16[16,128,128]{2,1,0:T(8,128)(2,1)S(1)}, u32[]{:S(2)}, u32[]{:S(2)}) %collective-permute-start) | collective-permute-done | bytes 524320 | tf_op jit(solution)/shard_map/ppermute | solution.py:192
  33.1 0.0 copy-done
  33.1 3.5 %attend.1 = bf16[4,128,512]{2,1,0:T(8,128)(2,1)S(1)} custom-call(s32[2,16,128]{2,1,0:T(8,128)S(1)} %copy-done, bf16[16,256,128]{2,1,0:T(8,128)(2,1)S(1)} %all_to_all.10.data_ref, bf16[16,128,128]{2,1,0:T(8,128)(2,1)S(1)} %collective-permute-done.other_ref), custom_call_target="tpu_custom_call" | custom-call | tf_op jit(solution)/shard_map/attend/pallas_call | solution.py:193
  36.5 11.6 %all_to_all.11.in_ref = bf16[4,128,512]{2,1,0:T(8,128)(2,1)S(1)} all-to-all(bf16[4,128,512]{2,1,0:T(8,128)(2,1)S(1)} %attend.1), channel_id=1, replica_groups={{0,4,8,12},{2,6,10,14},{16,20,24,28},{18,22,26,30},{1,5,9,13},{3,7,11,1..., dimensions={0} | all-to-all | bytes 1048576 | tf_op jit(solution)/shard_map/all_to_all | solution.py:206
  48.1 0.8 %unpack.1 = bf16[128,2048]{1,0:T(8,128)(2,1)} custom-call(bf16[4,128,512]{2,1,0:T(8,128)(2,1)S(1)} %all_to_all.11.in_ref), custom_call_target="tpu_custom_call" | custom-call | tf_op jit(solution)/shard_map/unpack/pallas_call | solution.py:207
  (1 shorter events, 0.0 us)
Async XLA Ops:
  28.4 4.7 %copy-start = (s32[2,16,128]{2,1,0:T(8,128)S(1)}, s32[2,16,128]{2,1,0:T(8,128)}, u32[]{:S(2)}) copy-start(s32[2,16,128]{2,1,0:T(8,128)} %get-tuple-element.7.rows_ref) | copy-start | bytes 49156
  28.5 4.6 %collective-permute-start = (bf16[16,128,128]{2,1,0:T(8,128)(2,1)S(1)}, bf16[16,128,128]{2,1,0:T(8,128)(2,1)S(1)}, u32[]{:S(2)}, u32[]{:S(2)}) collective-permute-start(bf16[16,128,128]{2,1,0:T(8,128)(2,1)S(1)} %slice.4), channel_id=1, source_target_pairs={{0,2},{2,0},{4,6},{6,4},{8,10},{10,8},{12,14},{14,12},{16,18},{18,... | collective-permute-start | bytes 1572872 | tf_op jit(solution)/shard_map/ppermute | solution.py:192

commit v4 on v2

--- a/solution.py
+++ b/solution.py
@@ -71,10 +71,12 @@
     for g in range(GROUPS):
         cols = slice(g * HEAD, (g + 1) * HEAD)
         keys = k_ref[:, cols]
-        vals = v_ref[:, cols].T
+        vals = v_ref[:, cols]
         for part in range(4):
             dest = (part // 2) * 8 + g * 2 + part % 2
-            out_ref[dest, 128:256, :] = vals if part % 2 else keys
+            half = slice(part % 2 * 64, part % 2 * 64 + 64)
+            out_ref[dest, 128:192, :] = keys[half]
+            out_ref[dest, 192:256, :] = vals[half]
     copies[5].wait()
     for g in range(GROUPS):
         wide = slice(g * GROUP_HEADS * HEAD, (g + 1) * GROUP_HEADS * HEAD)
@@ -87,55 +89,63 @@
                 ]
 
 
-def attend_kernel(rows_ref, data_ref, both_ref, out_ref, acc_ref):
-    key_at = lax.broadcasted_iota(jnp.int32, (TOK, TOK), 0)
+def attend_half(second, rows_ref, data_ref, half_ref, offset, sums_ref, peaks_ref, totals_ref, emit):
+    half = (lax.axis_index("ctx") + second) % 2
+    row = lax.broadcasted_iota(jnp.int32, (TOK, TOK), 0)
+    key_at = (row // 64) * TOK + row % 64 + half * 64
+
+    def keys(m):
+        return half_ref[2 * m : 2 * m + 2, offset : offset + 64, :].reshape(TOK, HEAD)
+
+    def values(m):
+        return half_ref[2 * m : 2 * m + 2, offset + 64 : offset + 128, :].reshape(TOK, HEAD).T
+
+    turned = [values(m) for m in range(CTX // 2)]
 
     def scores(pair):
-        shards = (2 * pair, 2 * pair + 1)
-        tiles = range(max(0, shards[0] - REACH), shards[1] + 1)
-        q = jnp.concatenate([data_ref[s, 0:128, :] for s in shards], 0)
-        kept = ({}, {})
+        tiles = range(max(0, pair - REACH // 2), pair + 1)
+        q = data_ref[2 * pair : 2 * pair + 2, 0:128, :].reshape(2 * TOK, HEAD)
+        kept = []
         peak = [None, None]
-        for kb in tiles:
-            both = dot(both_ref[0, kb], q, ROWS_BY_ROWS)
-            for i, s in enumerate(shards):
-                if not s - REACH <= kb <= s:
-                    continue
+        for m in tiles:
+            both = dot(keys(m), q, ROWS_BY_ROWS)
+            ones = []
+            for i in range(2):
+                s = 2 * pair + i
                 one = both[:, i * TOK : (i + 1) * TOK]
-                seen = key_at >= rows_ref[1, s : s + 1, :] - kb * TOK
-                if kb == s:
-                    seen = seen & (key_at <= rows_ref[0, s : s + 1, :] - kb * TOK)
+                seen = key_at >= rows_ref[1, s : s + 1, :] - m * 2 * TOK
+                if m == pair:
+                    seen = seen & (key_at <= rows_ref[0, s : s + 1, :] - m * 2 * TOK)
                 one = jnp.where(seen, one, MASKED)
-                kept[i][kb] = one
+                ones.append(one)
                 top = jnp.max(one.reshape(16, 8, TOK), axis=0)
                 peak[i] = top if peak[i] is None else jnp.maximum(peak[i], top)
-        return shards, tiles, kept, peak
+            kept.append(ones)
+        return pair, tiles, kept, peak
 
     def finish(state):
-        shards, tiles, kept, peak = state
-        weights, totals = [], []
+        pair, tiles, kept, peak = state
+        tops, totals = [], []
         for i in range(2):
             top = jnp.max(peak[i], axis=0, keepdims=True) * SCALE
-            total = jnp.zeros((8, TOK), jnp.float32)
-            rounded = {}
-            for kb, one in kept[i].items():
-                w = jnp.exp2(one * SCALE - top)
-                total = total + jnp.sum(w.reshape(16, 8, TOK), axis=0)
-                rounded[kb] = w.astype(jnp.bfloat16)
-            weights.append(rounded)
-            totals.append(jnp.sum(total, axis=0, keepdims=True))
-        none = jnp.zeros((TOK, TOK), jnp.bfloat16)
-        wide = jnp.concatenate(
-            [jnp.concatenate([weights[i].get(kb, none) for i in range(2)], 1) for kb in tiles], 0
+            if second:
+                top = jnp.maximum(top, peaks_ref[2 * pair + i : 2 * pair + i + 1, :])
+            tops.append(top)
+            totals.append(jnp.zeros((8, TOK), jnp.float32))
+        wide = []
+        for ones in kept:
+            parts = []
+            for i in range(2):
+                w = jnp.exp2(ones[i] * SCALE - tops[i])
+                totals[i] = totals[i] + jnp.sum(w.reshape(16, 8, TOK), axis=0)
+                parts.append(w.astype(jnp.bfloat16))
+            wide.append(jnp.concatenate(parts, 1))
+        mixed = dot(
+            jnp.concatenate([turned[m] for m in tiles], 1), jnp.concatenate(wide, 0), ROWS_BY_COLS
         )
-        vals = jnp.concatenate([both_ref[1, kb] for kb in tiles], 1)
-        mixed = dot(vals, wide, ROWS_BY_COLS)
-        for i, s in enumerate(shards):
-            rows = (mixed[:, i * TOK : (i + 1) * TOK] * (1.0 / totals[i])).T
-            for h in range(GROUP_HEADS):
-                for y in range(4):
-                    at = h * PART + y * BR
-                    acc_ref[y, s * BR : (s + 1) * BR, h * HEAD : (h + 1) * HEAD] = rows[at : at + BR]
+        for i in range(2):
+            total = jnp.sum(totals[i], axis=0, keepdims=True)
+            emit(2 * pair + i, mixed[:, i * TOK : (i + 1) * TOK], tops[i], total)
 
     ahead = scores(0)
     for pair in range(1, CTX // 2):
@@ -143,6 +153,28 @@
         finish(ahead)
         ahead = following
     finish(ahead)
+
+
+def own_kernel(rows_ref, data_ref, sums_ref, peaks_ref, totals_ref):
+    def emit(s, mixed, top, total):
+        sums_ref[s] = mixed
+        peaks_ref[s : s + 1, :] = top
+        totals_ref[s : s + 1, :] = total
+
+    attend_half(0, rows_ref, data_ref, data_ref, TOK, None, None, None, emit)
+
+
+def other_kernel(rows_ref, data_ref, other_ref, sums_ref, peaks_ref, totals_ref, out_ref, acc_ref):
+    def emit(s, mixed, top, total):
+        shrink = jnp.exp2(peaks_ref[s : s + 1, :] - top)
+        total = total + totals_ref[s : s + 1, :] * shrink
+        rows = ((mixed + sums_ref[s] * shrink) * (1.0 / total)).T
+        for h in range(GROUP_HEADS):
+            for y in range(4):
+                at = h * PART + y * BR
+                acc_ref[y, s * BR : (s + 1) * BR, h * HEAD : (h + 1) * HEAD] = rows[at : at + BR]
+
+    attend_half(1, rows_ref, data_ref, other_ref, 0, sums_ref, peaks_ref, totals_ref, emit)
     out_ref[...] = acc_ref[...].astype(jnp.bfloat16)
 
 
@@ -184,17 +216,29 @@
         name="pack",
     )(owner_map, doc_lengths, queries, keys, values)
     data = lax.all_to_all(packed, "ctx", 0, 0, tiled=True)
-    chips = [[2 * i, 2 * i + 1] for i in range(CTX // 2)]
-    both = lax.all_gather(data[:, TOK:], "ctx", axis=0, axis_index_groups=chips)
+    other = lax.ppermute(data[:, TOK:], "ctx", [(i, i ^ 1) for i in range(CTX)])
+    sums, peaks, totals = pl.pallas_call(
+        own_kernel,
+        out_shape=(
+            jax.ShapeDtypeStruct((CTX, HEAD, TOK), jnp.float32),
+            jax.ShapeDtypeStruct((CTX, TOK), jnp.float32),
+            jax.ShapeDtypeStruct((CTX, TOK), jnp.float32),
+        ),
+        in_specs=[VMEM] * 2,
+        out_specs=(VMEM,) * 3,
+        compiler_params=pltpu.CompilerParams(vmem_limit_bytes=40 << 20),
+        cost_estimate=pl.CostEstimate(flops=10**9, bytes_accessed=3 << 20, transcendentals=10**6),
+        name="own_half",
+    )(rows, data)
     mixed = pl.pallas_call(
-        attend_kernel,
+        other_kernel,
         out_shape=jax.ShapeDtypeStruct((4, TOK, GROUP_HEADS * HEAD), jnp.bfloat16),
-        in_specs=[VMEM, VMEM, VMEM],
+        in_specs=[VMEM] * 6,
         out_specs=VMEM,
         scratch_shapes=[pltpu.VMEM((4, TOK, GROUP_HEADS * HEAD), jnp.float32)],
         compiler_params=pltpu.CompilerParams(vmem_limit_bytes=40 << 20),
-        name="attend",
-    )(rows, data, both)
+        name="other_half",
+    )(rows, data, other, sums, peaks, totals)
     rings = [[x * 8 + y * 2 + c for y in range(4)] for x in range(2) for c in range(2)]
     back = lax.all_to_all(mixed, "ctx", 0, 0, tiled=True, axis_index_groups=rings)
     return pl.pallas_call(

time: 80.3 us -> 48.3 us (0.60)
  waiting for transfers between devices: 20.1 us -> 0.01 us
  between operations: 13.4 us -> 0.05 us
  starting transfers between devices: 0.01 us -> 3.07 us
  local copies, waits for them, and re-layouts: 2.06 us -> 0.04 us
    all_gather x1 -> x0, waiting for transfers between devices: 20.1 us -> none  [body(): both = lax.all_gather(data[:, TOK:], 'ctx', axis=0, axis_index_groups=chips)]
    ppermute x0 -> x1, starting transfers between devices: none -> 3.07 us  [body(): other = lax.ppermute(data[:, TOK:], 'ctx', [(i, i ^ 1) for i in range(CTX)])]
    unnamed x4 -> x2, local copies, waits for them, and re-layouts: 1.23 us -> 0.01 us
    pallas_call x1 -> x2, Pallas kernels: 3.31 us -> 3.94 us  [the longest x1 2.04 us: body(): pl.pallas_call(other_kernel, out_shape=jax.ShapeDtypeStruct((4, TOK, GROU...]
  transfers between devices with their start and end apart: 1 -> 1, of which waited for: 1 -> 0; matrix products, arithmetic and copies ran while one was open for 0% -> 0% of each run, Pallas kernels for 0% -> 4%
where the time goes in v4:
time: 48.3 us; the launch traced here: 48 us
  blocking collectives  37.6 us (78%)
  Pallas kernels  7.29 us (15%)
  starting transfers between devices  3.07 us (6%)
    all_to_all x1, blocking collectives, body(): data = lax.all_to_all(packed, 'ctx', 0, 0, tiled=True)  25.8 us
    all_to_all x1, blocking collectives, body(): lax.all_to_all(mixed, 'ctx', 0, 0, tiled=True, axis_index_groups=rings)  11.7 us
    ppermute x1, starting transfers between devices, body(): other = lax.ppermute(data[:, TOK:], 'ctx', [(i, i ^ 1) for i in range(CTX)])  3.07 us
    pallas_call x1, Pallas kernels, body(): pl.pallas_call(pack_kernel, out_shape=(jax.ShapeDtypeStruct((CTX, CHUNK,...  2.53 us
    pallas_call x1, Pallas kernels, body(): pl.pallas_call(other_kernel, out_shape=jax.ShapeDtypeStruct((4, TOK, GROU...  2.04 us
    pallas_call x1, Pallas kernels, body(): pl.pallas_call(own_kernel, out_shape=(jax.ShapeDtypeStruct((CTX, HEAD, TO...  1.9 us
  transfers between devices with their start and end apart: 1, of which 0 were waited for; matrix products, arithmetic and copies ran while one was open for 0% of the time, Pallas kernels for 4%

profile of v4, /device:TPU:1, one launch (start us, length us, event | category | flops | bytes accessed | tf_op | source)
XLA Modules:
  0.0 48.0 jit_solution(15703794711514572595)
XLA Ops:
  0.0 2.5 %pack.1 = (bf16[16,256,128]{2,1,0:T(8,128)(2,1)}, s32[2,16,128]{2,1,0:T(8,128)}) custom-call(s32[16,16]{1,0:T(8,128)} %owner_any.1, s32[16]{0:T(128)} %doc_any.1, bf16[128,2048]{1,0:T(8,128)(2,1)} %q_any.1, bf16[128,512]{1,0:T(8,128)(2,1)} %k_any.1, bf16[128,512]{1,0:T(8,128)(2,1)} %v_any.1), custom_call_target="tpu_custom_call" | custom-call | tf_op jit(solution)/shard_map/pack/pallas_call | solution.py:198
  2.5 25.8 %all_to_all.10.data_ref = bf16[16,256,128]{2,1,0:T(8,128)(2,1)S(1)} all-to-all(bf16[16,256,128]{2,1,0:T(8,128)(2,1)} %get-tuple-element.11), channel_id=1, replica_groups=mesh['dp'=16,'ctx'=16,'head'=2] {'ctx'}, dimensions={0} | all-to-all | bytes 2097152 | tf_op jit(solution)/shard_map/all_to_all | solution.py:218
  28.3 0.0 copy-start
  28.4 3.1 %collective-permute-start = (bf16[16,128,128]{2,1,0:T(8,128)(2,1)S(1)}, bf16[16,128,128]{2,1,0:T(8,128)(2,1)S(1)}, u32[]{:S(2)}, u32[]{:S(2)}) collective-permute-start(bf16[16,128,128]{2,1,0:T(8,128)(2,1)S(1)} %slice.4), channel_id=1, source_target_pairs={{0,2},{2,0},{4,6},{6,4},{8,10},{10,8},{12,14},{14,12},{16,18},{18,... | collective-permute-start | bytes 1572872 | tf_op jit(solution)/shard_map/ppermute | solution.py:219
  31.5 0.0 copy-done
  31.5 1.9 %own_half.1 = (f32[16,128,128]{2,1,0:T(8,128)S(1)}, f32[16,128]{1,0:T(8,128)S(1)}, f32[16,128]{1,0:T(8,128)S(1)}) custom-call(s32[2,16,128]{2,1,0:T(8,128)S(1)} %copy-done, bf16[16,256,128]{2,1,0:T(8,128)(2,1)S(1)} %all_to_all.10.data_ref), custom_call_target="tpu_custom_call" | custom-call | flops 1000000000 | bytes 3145728 | tf_op jit(solution)/shard_map/own_half/pallas_call | solution.py:220
  33.4 0.0 collective-permute-done.other_ref
  33.4 2.0 %other_half.1 = bf16[4,128,512]{2,1,0:T(8,128)(2,1)S(1)} custom-call(s32[2,16,128]{2,1,0:T(8,128)S(1)} %copy-done, bf16[16,256,128]{2,1,0:T(8,128)(2,1)S(1)} %all_to_all.10.data_ref, bf16[16,128,128]{2,1,0:T(8,128)(2,1)S(1)} %collective-permute-done.other_ref, f32[16,128,128]{2,1,0:T(8,128)S(1)} %get-tuple-element.12.sums_ref, ...), custom_call_target="tpu_custom_call" | custom-call | tf_op jit(solution)/shard_map/other_half/pallas_call | solution.py:233
  35.5 11.7 %all_to_all.11.in_ref = bf16[4,128,512]{2,1,0:T(8,128)(2,1)S(1)} all-to-all(bf16[4,128,512]{2,1,0:T(8,128)(2,1)S(1)} %other_half.1), channel_id=1, replica_groups={{0,4,8,12},{2,6,10,14},{16,20,24,28},{18,22,26,30},{1,5,9,13},{3,7,11,1..., dimensions={0} | all-to-all | bytes 1048576 | tf_op jit(solution)/shard_map/all_to_all | solution.py:243
  47.2 0.8 %unpack.1 = bf16[128,2048]{1,0:T(8,128)(2,1)} custom-call(bf16[4,128,512]{2,1,0:T(8,128)(2,1)S(1)} %all_to_all.11.in_ref), custom_call_target="tpu_custom_call" | custom-call | tf_op jit(solution)/shard_map/unpack/pallas_call | solution.py:244
  (1 shorter events, 0.0 us)
Async XLA Ops:
  28.3 3.1 %copy-start = (s32[2,16,128]{2,1,0:T(8,128)S(1)}, s32[2,16,128]{2,1,0:T(8,128)}, u32[]{:S(2)}) copy-start(s32[2,16,128]{2,1,0:T(8,128)} %get-tuple-element.10.rows_ref) | copy-start | bytes 49156
  28.4 5.0 %collective-permute-start = (bf16[16,128,128]{2,1,0:T(8,128)(2,1)S(1)}, bf16[16,128,128]{2,1,0:T(8,128)(2,1)S(1)}, u32[]{:S(2)}, u32[]{:S(2)}) collective-permute-start(bf16[16,128,128]{2,1,0:T(8,128)(2,1)S(1)} %slice.4), channel_id=1, source_target_pairs={{0,2},{2,0},{4,6},{6,4},{8,10},{10,8},{12,14},{14,12},{16,18},{18,... | collective-permute-start | bytes 1572872 | tf_op jit(solution)/shard_map/ppermute | solution.py:219

commit v5 on v4

--- a/solution.py
+++ b/solution.py
@@ -195,6 +195,10 @@
 
 
 def body(queries, keys, values, doc_lengths, owner_map):
+    here = [
+        pltpu.with_memory_space_constraint(a, pltpu.HBM)
+        for a in (owner_map, doc_lengths, queries, keys, values)
+    ]
     packed, rows = pl.pallas_call(
         pack_kernel,
         out_shape=(
@@ -212,9 +216,9 @@
             pltpu.VMEM(values.shape, jnp.bfloat16),
             pltpu.SemaphoreType.DMA((6,)),
         ],
-        compiler_params=pltpu.CompilerParams(vmem_limit_bytes=60 << 20),
+        compiler_params=pltpu.CompilerParams(vmem_limit_bytes=24 << 20),
         name="pack",
-    )(owner_map, doc_lengths, queries, keys, values)
+    )(*here)
     data = lax.all_to_all(packed, "ctx", 0, 0, tiled=True)
     other = lax.ppermute(data[:, TOK:], "ctx", [(i, i ^ 1) for i in range(CTX)])
     sums, peaks, totals = pl.pallas_call(

time: 48.3 us -> 46.2 us (0.957)
  blocking collectives: 37.6 us -> 36.6 us
  Pallas kernels: 7.29 us -> 6.31 us
    all_to_all x1, blocking collectives: 25.8 us -> 24.8 us  [body(): data = lax.all_to_all(packed, 'ctx', 0, 0, tiled=True)]
    pallas_call x1, Pallas kernels: 2.53 us -> 1.56 us  [body(): pl.pallas_call(pack_kernel, out_shape=(jax.ShapeDtypeStruct((CTX, CHUNK,...]
where the time goes in v5:
time: 46.2 us; the launch traced here: 46 us
  blocking collectives  36.6 us (79%)
  Pallas kernels  6.31 us (14%)
  starting transfers between devices  3.07 us (7%)
    all_to_all x1, blocking collectives, body(): data = lax.all_to_all(packed, 'ctx', 0, 0, tiled=True)  24.8 us
    all_to_all x1, blocking collectives, body(): lax.all_to_all(mixed, 'ctx', 0, 0, tiled=True, axis_index_groups=rings)  11.7 us
    ppermute x1, starting transfers between devices, body(): other = lax.ppermute(data[:, TOK:], 'ctx', [(i, i ^ 1) for i in range(CTX)])  3.07 us
    pallas_call x1, Pallas kernels, body(): pl.pallas_call(other_kernel, out_shape=jax.ShapeDtypeStruct((4, TOK, GROU...  2.04 us
    pallas_call x1, Pallas kernels, body(): pl.pallas_call(own_kernel, out_shape=(jax.ShapeDtypeStruct((CTX, HEAD, TO...  1.89 us
    pallas_call x1, Pallas kernels, body(): pl.pallas_call(pack_kernel, out_shape=(jax.ShapeDtypeStruct((CTX, CHUNK,...  1.56 us
  transfers between devices with their start and end apart: 1, of which 0 were waited for; matrix products, arithmetic and copies ran while one was open for 0% of the time, Pallas kernels for 4%

profile of v5, /device:TPU:1, one launch (start us, length us, event | category | flops | bytes accessed | tf_op | source)
XLA Modules:
  0.0 46.0 jit_solution(15231388110774297627)
XLA Ops:
  0.0 1.6 %pack.1 = (bf16[16,256,128]{2,1,0:T(8,128)(2,1)S(1)}, s32[2,16,128]{2,1,0:T(8,128)S(1)}) custom-call(s32[16,16]{1,0:T(8,128)} %owner_any.1, s32[16]{0:T(128)} %doc_any.1, bf16[128,2048]{1,0:T(8,128)(2,1)} %q_any.1, bf16[128,512]{1,0:T(8,128)(2,1)} %k_any.1, bf16[128,512]{1,0:T(8,128)(2,1)} %v_any.1), custom_call_target="tpu_custom_call" | custom-call | tf_op jit(solution)/shard_map/pack/pallas_call | solution.py:202
  1.6 24.8 %all_to_all.10.data_ref = bf16[16,256,128]{2,1,0:T(8,128)(2,1)S(1)} all-to-all(bf16[16,256,128]{2,1,0:T(8,128)(2,1)S(1)} %get-tuple-element.11), channel_id=1, replica_groups=mesh['dp'=16,'ctx'=16,'head'=2] {'ctx'}, dimensions={0} | all-to-all | bytes 2097152 | tf_op jit(solution)/shard_map/all_to_all | solution.py:222
  26.4 3.1 %collective-permute-start = (bf16[16,128,128]{2,1,0:T(8,128)(2,1)S(1)}, bf16[16,128,128]{2,1,0:T(8,128)(2,1)S(1)}, u32[]{:S(2)}, u32[]{:S(2)}) collective-permute-start(bf16[16,128,128]{2,1,0:T(8,128)(2,1)S(1)} %slice.4), channel_id=1, source_target_pairs={{0,2},{2,0},{4,6},{6,4},{8,10},{10,8},{12,14},{14,12},{16,18},{18,... | collective-permute-start | bytes 1572872 | tf_op jit(solution)/shard_map/ppermute | solution.py:223
  29.5 1.9 %own_half.1 = (f32[16,128,128]{2,1,0:T(8,128)S(1)}, f32[16,128]{1,0:T(8,128)S(1)}, f32[16,128]{1,0:T(8,128)S(1)}) custom-call(s32[2,16,128]{2,1,0:T(8,128)S(1)} %get-tuple-element.10.rows_ref, bf16[16,256,128]{2,1,0:T(8,128)(2,1)S(1)} %all_to_all.10.data_ref), custom_call_target="tpu_custom_call" | custom-call | flops 1000000000 | bytes 3145728 | tf_op jit(solution)/shard_map/own_half/pallas_call | solution.py:224
  31.4 0.0 collective-permute-done.other_ref
  31.4 2.0 %other_half.1 = bf16[4,128,512]{2,1,0:T(8,128)(2,1)S(1)} custom-call(s32[2,16,128]{2,1,0:T(8,128)S(1)} %get-tuple-element.10.rows_ref, bf16[16,256,128]{2,1,0:T(8,128)(2,1)S(1)} %all_to_all.10.data_ref, bf16[16,128,128]{2,1,0:T(8,128)(2,1)S(1)} %collective-permute-done.other_ref, f32[16,128,128]{2,1,0:T(8,128)S(1)} %get-tuple-element.12.sums_ref, ...), custom_call_target="tpu_custom_call" | custom-call | tf_op jit(solution)/shard_map/other_half/pallas_call | solution.py:237
  33.5 11.7 %all_to_all.11.in_ref = bf16[4,128,512]{2,1,0:T(8,128)(2,1)S(1)} all-to-all(bf16[4,128,512]{2,1,0:T(8,128)(2,1)S(1)} %other_half.1), channel_id=1, replica_groups={{0,4,8,12},{2,6,10,14},{16,20,24,28},{18,22,26,30},{1,5,9,13},{3,7,11,1..., dimensions={0} | all-to-all | bytes 1048576 | tf_op jit(solution)/shard_map/all_to_all | solution.py:247
  45.2 0.8 %unpack.1 = bf16[128,2048]{1,0:T(8,128)(2,1)} custom-call(bf16[4,128,512]{2,1,0:T(8,128)(2,1)S(1)} %all_to_all.11.in_ref), custom_call_target="tpu_custom_call" | custom-call | tf_op jit(solution)/shard_map/unpack/pallas_call | solution.py:248
  (1 shorter events, 0.0 us)
Async XLA Ops:
  26.4 5.0 %collective-permute-start = (bf16[16,128,128]{2,1,0:T(8,128)(2,1)S(1)}, bf16[16,128,128]{2,1,0:T(8,128)(2,1)S(1)}, u32[]{:S(2)}, u32[]{:S(2)}) collective-permute-start(bf16[16,128,128]{2,1,0:T(8,128)(2,1)S(1)} %slice.4), channel_id=1, source_target_pairs={{0,2},{2,0},{4,6},{6,4},{8,10},{10,8},{12,14},{14,12},{16,18},{18,... | collective-permute-start | bytes 1572872 | tf_op jit(solution)/shard_map/ppermute | solution.py:223

commit v6 on v5

--- a/solution.py
+++ b/solution.py
@@ -18,6 +18,10 @@
 REACH = 8
 CHUNK = 256
 MASKED = -1e30
+ORDER = [5, 6, 10, 11, 8, 4, 7, 0, 1, 15, 2, 3, 13, 14, 9, 12]
+PLACE = [ORDER.index(i) for i in range(CTX)]
+RING = [2, 0, 3, 1]
+SPOT = [RING.index(y) for y in range(4)]
 SCALE = math.log2(math.e) / math.sqrt(HEAD)
 ROWS_BY_ROWS = (((1,), (1,)), ((), ()))
 ROWS_BY_COLS = (((1,), (0,)), ((), ()))
@@ -73,7 +77,7 @@
         keys = k_ref[:, cols]
         vals = v_ref[:, cols]
         for part in range(4):
-            dest = (part // 2) * 8 + g * 2 + part % 2
+            dest = PLACE[(part // 2) * 8 + g * 2 + part % 2]
             half = slice(part % 2 * 64, part % 2 * 64 + 64)
             out_ref[dest, 128:192, :] = keys[half]
             out_ref[dest, 192:256, :] = vals[half]
@@ -82,7 +86,7 @@
         wide = slice(g * GROUP_HEADS * HEAD, (g + 1) * GROUP_HEADS * HEAD)
         moved = dot(order, q_ref[:, wide], ROWS_BY_COLS).astype(jnp.bfloat16)
         for part in range(4):
-            dest = (part // 2) * 8 + g * 2 + part % 2
+            dest = PLACE[(part // 2) * 8 + g * 2 + part % 2]
             for h in range(GROUP_HEADS):
                 out_ref[dest, h * PART : (h + 1) * PART, :] = moved[
                     part * PART : (part + 1) * PART, h * HEAD : (h + 1) * HEAD
@@ -94,17 +98,20 @@
     row = lax.broadcasted_iota(jnp.int32, (TOK, TOK), 0)
     key_at = (row // 64) * TOK + row % 64 + half * 64
 
+    def two(ref, m, low, high):
+        return jnp.concatenate([ref[PLACE[2 * m], low:high, :], ref[PLACE[2 * m + 1], low:high, :]], 0)
+
     def keys(m):
-        return half_ref[2 * m : 2 * m + 2, offset : offset + 64, :].reshape(TOK, HEAD)
+        return two(half_ref, m, offset, offset + 64)
 
     def values(m):
-        return half_ref[2 * m : 2 * m + 2, offset + 64 : offset + 128, :].reshape(TOK, HEAD).T
+        return two(half_ref, m, offset + 64, offset + 128).T
 
     turned = [values(m) for m in range(CTX // 2)]
 
     def scores(pair):
         tiles = range(max(0, pair - REACH // 2), pair + 1)
-        q = data_ref[2 * pair : 2 * pair + 2, 0:128, :].reshape(2 * TOK, HEAD)
+        q = two(data_ref, pair, 0, 128)
         kept = []
         peak = [None, None]
         for m in tiles:
@@ -172,7 +179,7 @@
         for h in range(GROUP_HEADS):
             for y in range(4):
                 at = h * PART + y * BR
-                acc_ref[y, s * BR : (s + 1) * BR, h * HEAD : (h + 1) * HEAD] = rows[at : at + BR]
+                acc_ref[SPOT[y], s * BR : (s + 1) * BR, h * HEAD : (h + 1) * HEAD] = rows[at : at + BR]
 
     attend_half(1, rows_ref, data_ref, other_ref, 0, sums_ref, peaks_ref, totals_ref, emit)
     out_ref[...] = acc_ref[...].astype(jnp.bfloat16)
@@ -181,7 +188,7 @@
 def unpack_kernel(in_ref, out_any, sems):
     wide = GROUP_HEADS * HEAD
     copies = [
-        pltpu.make_async_copy(in_ref.at[g], out_any.at[:, g * wide : (g + 1) * wide], sems.at[g])
+        pltpu.make_async_copy(in_ref.at[SPOT[g]], out_any.at[:, g * wide : (g + 1) * wide], sems.at[g])
         for g in range(GROUPS)
     ]
     for copy in copies:
@@ -219,7 +226,7 @@
         compiler_params=pltpu.CompilerParams(vmem_limit_bytes=24 << 20),
         name="pack",
     )(*here)
-    data = lax.all_to_all(packed, "ctx", 0, 0, tiled=True)
+    data = lax.all_to_all(packed, "ctx", 0, 0, tiled=True, axis_index_groups=[ORDER])
     other = lax.ppermute(data[:, TOK:], "ctx", [(i, i ^ 1) for i in range(CTX)])
     sums, peaks, totals = pl.pallas_call(
         own_kernel,
@@ -243,7 +250,7 @@
         compiler_params=pltpu.CompilerParams(vmem_limit_bytes=40 << 20),
         name="other_half",
     )(rows, data, other, sums, peaks, totals)
-    rings = [[x * 8 + y * 2 + c for y in range(4)] for x in range(2) for c in range(2)]
+    rings = [[x * 8 + y * 2 + c for y in RING] for x in range(2) for c in range(2)]
     back = lax.all_to_all(mixed, "ctx", 0, 0, tiled=True, axis_index_groups=rings)
     return pl.pallas_call(
         unpack_kernel,

time: 46.2 us -> 44.5 us (0.963)
  starting transfers between devices: 3.07 us -> 1.92 us
  blocking collectives: 36.6 us -> 36 us
    ppermute x1, starting transfers between devices: 3.07 us -> 1.92 us  [body(): other = lax.ppermute(data[:, TOK:], 'ctx', [(i, i ^ 1) for i in range(CTX)])]
    all_to_all x1, blocking collectives: 24.8 us -> 24 us  [body(): lax.all_to_all(packed, 'ctx', 0, 0, tiled=True, axis_index_groups=[ORDER])]
where the time goes in v6:
time: 44.5 us; the launch traced here: 44.3 us
  blocking collectives  36 us (81%)
  Pallas kernels  6.31 us (14%)
  starting transfers between devices  1.92 us (4%)
    all_to_all x1, blocking collectives, body(): lax.all_to_all(packed, 'ctx', 0, 0, tiled=True, axis_index_groups=[ORDER])  24 us
    all_to_all x1, blocking collectives, body(): lax.all_to_all(mixed, 'ctx', 0, 0, tiled=True, axis_index_groups=rings)  11.9 us
    pallas_call x1, Pallas kernels, body(): pl.pallas_call(other_kernel, out_shape=jax.ShapeDtypeStruct((4, TOK, GROU...  2.04 us
    ppermute x1, starting transfers between devices, body(): other = lax.ppermute(data[:, TOK:], 'ctx', [(i, i ^ 1) for i in range(CTX)])  1.92 us
    pallas_call x1, Pallas kernels, body(): pl.pallas_call(own_kernel, out_shape=(jax.ShapeDtypeStruct((CTX, HEAD, TO...  1.89 us
    pallas_call x1, Pallas kernels, body(): pl.pallas_call(pack_kernel, out_shape=(jax.ShapeDtypeStruct((CTX, CHUNK,...  1.56 us
  transfers between devices with their start and end apart: 1, of which 0 were waited for; matrix products, arithmetic and copies ran while one was open for 0% of the time, Pallas kernels for 4%

profile of v6, /device:TPU:1, one launch (start us, length us, event | category | flops | bytes accessed | tf_op | source)
XLA Modules:
  0.0 44.3 jit_solution(16911817265630616985)
XLA Ops:
  0.0 1.6 %pack.1 = (bf16[16,256,128]{2,1,0:T(8,128)(2,1)S(1)}, s32[2,16,128]{2,1,0:T(8,128)S(1)}) custom-call(s32[16,16]{1,0:T(8,128)} %owner_any.1, s32[16]{0:T(128)} %doc_any.1, bf16[128,2048]{1,0:T(8,128)(2,1)} %q_any.1, bf16[128,512]{1,0:T(8,128)(2,1)} %k_any.1, bf16[128,512]{1,0:T(8,128)(2,1)} %v_any.1), custom_call_target="tpu_custom_call" | custom-call | tf_op jit(solution)/shard_map/pack/pallas_call | solution.py:209
  1.6 24.0 %all_to_all.10.data_ref = bf16[16,256,128]{2,1,0:T(8,128)(2,1)S(1)} all-to-all(bf16[16,256,128]{2,1,0:T(8,128)(2,1)S(1)} %get-tuple-element.11), channel_id=1, replica_groups={{10,12,20,22,16,8,14,0,2,30,4,6,26,28,18,24},{11,13,21,23,17,9,15,1,3,3..., dimensions={0} | all-to-all | bytes 2097152 | tf_op jit(solution)/shard_map/all_to_all | solution.py:229
  25.7 1.9 %collective-permute-start = (bf16[16,128,128]{2,1,0:T(8,128)(2,1)S(1)}, bf16[16,128,128]{2,1,0:T(8,128)(2,1)S(1)}, u32[]{:S(2)}, u32[]{:S(2)}) collective-permute-start(bf16[16,128,128]{2,1,0:T(8,128)(2,1)S(1)} %slice.4), channel_id=1, source_target_pairs={{0,2},{2,0},{4,6},{6,4},{8,10},{10,8},{12,14},{14,12},{16,18},{18,... | collective-permute-start | bytes 1572872 | tf_op jit(solution)/shard_map/ppermute | solution.py:230
  27.6 1.9 %own_half.1 = (f32[16,128,128]{2,1,0:T(8,128)S(1)}, f32[16,128]{1,0:T(8,128)S(1)}, f32[16,128]{1,0:T(8,128)S(1)}) custom-call(s32[2,16,128]{2,1,0:T(8,128)S(1)} %get-tuple-element.10.rows_ref, bf16[16,256,128]{2,1,0:T(8,128)(2,1)S(1)} %all_to_all.10.data_ref), custom_call_target="tpu_custom_call" | custom-call | flops 1000000000 | bytes 3145728 | tf_op jit(solution)/shard_map/own_half/pallas_call | solution.py:231
  29.5 0.0 collective-permute-done.other_ref
  29.5 2.0 %other_half.1 = bf16[4,128,512]{2,1,0:T(8,128)(2,1)S(1)} custom-call(s32[2,16,128]{2,1,0:T(8,128)S(1)} %get-tuple-element.10.rows_ref, bf16[16,256,128]{2,1,0:T(8,128)(2,1)S(1)} %all_to_all.10.data_ref, bf16[16,128,128]{2,1,0:T(8,128)(2,1)S(1)} %collective-permute-done.other_ref, f32[16,128,128]{2,1,0:T(8,128)S(1)} %get-tuple-element.12.sums_ref, ...), custom_call_target="tpu_custom_call" | custom-call | tf_op jit(solution)/shard_map/other_half/pallas_call | solution.py:244
  31.5 11.9 %all_to_all.11.in_ref = bf16[4,128,512]{2,1,0:T(8,128)(2,1)S(1)} all-to-all(bf16[4,128,512]{2,1,0:T(8,128)(2,1)S(1)} %other_half.1), channel_id=1, replica_groups={{8,0,12,4},{10,2,14,6},{24,16,28,20},{26,18,30,22},{9,1,13,5},{11,3,15,..., dimensions={0} | all-to-all | bytes 1048576 | tf_op jit(solution)/shard_map/all_to_all | solution.py:254
  43.5 0.8 %unpack.1 = bf16[128,2048]{1,0:T(8,128)(2,1)} custom-call(bf16[4,128,512]{2,1,0:T(8,128)(2,1)S(1)} %all_to_all.11.in_ref), custom_call_target="tpu_custom_call" | custom-call | tf_op jit(solution)/shard_map/unpack/pallas_call | solution.py:255
  (1 shorter events, 0.0 us)
Async XLA Ops:
  25.7 3.8 %collective-permute-start = (bf16[16,128,128]{2,1,0:T(8,128)(2,1)S(1)}, bf16[16,128,128]{2,1,0:T(8,128)(2,1)S(1)}, u32[]{:S(2)}, u32[]{:S(2)}) collective-permute-start(bf16[16,128,128]{2,1,0:T(8,128)(2,1)S(1)} %slice.4), channel_id=1, source_target_pairs={{0,2},{2,0},{4,6},{6,4},{8,10},{10,8},{12,14},{14,12},{16,18},{18,... | collective-permute-start | bytes 1572872 | tf_op jit(solution)/shard_map/ppermute | solution.py:230

commit v7 on v6

--- a/solution.py
+++ b/solution.py
@@ -109,6 +109,13 @@
 
     turned = [values(m) for m in range(CTX // 2)]
 
+    def reached(pair, m, i):
+        if m == pair and i == 0:
+            return slice(0, 64)
+        if m == pair - REACH // 2 and i == 1:
+            return slice(64, TOK)
+        return slice(0, TOK)
+
     def scores(pair):
         tiles = range(max(0, pair - REACH // 2), pair + 1)
         q = two(data_ref, pair, 0, 128)
@@ -119,13 +126,14 @@
             ones = []
             for i in range(2):
                 s = 2 * pair + i
-                one = both[:, i * TOK : (i + 1) * TOK]
-                seen = key_at >= rows_ref[1, s : s + 1, :] - m * 2 * TOK
+                part = reached(pair, m, i)
+                one = both[part, i * TOK : (i + 1) * TOK]
+                seen = key_at[part] >= rows_ref[1, s : s + 1, :] - m * 2 * TOK
                 if m == pair:
-                    seen = seen & (key_at <= rows_ref[0, s : s + 1, :] - m * 2 * TOK)
+                    seen = seen & (key_at[part] <= rows_ref[0, s : s + 1, :] - m * 2 * TOK)
                 one = jnp.where(seen, one, MASKED)
                 ones.append(one)
-                top = jnp.max(one.reshape(16, 8, TOK), axis=0)
+                top = jnp.max(one.reshape(-1, 8, TOK), axis=0)
                 peak[i] = top if peak[i] is None else jnp.maximum(peak[i], top)
             kept.append(ones)
         return pair, tiles, kept, peak
@@ -140,12 +148,19 @@
             tops.append(top)
             totals.append(jnp.zeros((8, TOK), jnp.float32))
         wide = []
-        for ones in kept:
+        none = jnp.zeros((64, TOK), jnp.bfloat16)
+        for m, ones in zip(tiles, kept):
             parts = []
             for i in range(2):
                 w = jnp.exp2(ones[i] * SCALE - tops[i])
-                totals[i] = totals[i] + jnp.sum(w.reshape(16, 8, TOK), axis=0)
-                parts.append(w.astype(jnp.bfloat16))
+                totals[i] = totals[i] + jnp.sum(w.reshape(-1, 8, TOK), axis=0)
+                w = w.astype(jnp.bfloat16)
+                part = reached(pair, m, i)
+                if part.start > 0:
+                    w = jnp.concatenate([none, w], 0)
+                if part.stop < TOK:
+                    w = jnp.concatenate([w, none], 0)
+                parts.append(w)
             wide.append(jnp.concatenate(parts, 1))
         mixed = dot(
             jnp.concatenate([turned[m] for m in tiles], 1), jnp.concatenate(wide, 0), ROWS_BY_COLS

time: 44.5 us -> 44.2 us (level)
  transfers between devices with their start and end apart: 1 -> 1, of which waited for: 0 -> 1; matrix products, arithmetic and copies ran while one was open for 0% -> 0% of each run, Pallas kernels for 4% -> 4%
where the time goes in v7:
time: 44.2 us; the launch traced here: 44 us
  blocking collectives  35.9 us (81%)
  Pallas kernels  6.04 us (14%)
  starting transfers between devices  1.92 us (4%)
    all_to_all x1, blocking collectives, body(): lax.all_to_all(packed, 'ctx', 0, 0, tiled=True, axis_index_groups=[ORDER])  24 us
    all_to_all x1, blocking collectives, body(): lax.all_to_all(mixed, 'ctx', 0, 0, tiled=True, axis_index_groups=rings)  11.8 us
    ppermute x1, starting transfers between devices, body(): other = lax.ppermute(data[:, TOK:], 'ctx', [(i, i ^ 1) for i in range(CTX)])  1.92 us
    pallas_call x1, Pallas kernels, body(): pl.pallas_call(other_kernel, out_shape=jax.ShapeDtypeStruct((4, TOK, GROU...  1.88 us
    pallas_call x1, Pallas kernels, body(): pl.pallas_call(own_kernel, out_shape=(jax.ShapeDtypeStruct((CTX, HEAD, TO...  1.78 us
    pallas_call x1, Pallas kernels, body(): pl.pallas_call(pack_kernel, out_shape=(jax.ShapeDtypeStruct((CTX, CHUNK,...  1.56 us
  transfers between devices with their start and end apart: 1, of which 1 were waited for; matrix products, arithmetic and copies ran while one was open for 0% of the time, Pallas kernels for 4%

profile of v7, /device:TPU:1, one launch (start us, length us, event | category | flops | bytes accessed | tf_op | source)
XLA Modules:
  0.0 44.0 jit_solution(15680150677309047083)
XLA Ops:
  0.0 1.6 %pack.1 = (bf16[16,256,128]{2,1,0:T(8,128)(2,1)S(1)}, s32[2,16,128]{2,1,0:T(8,128)S(1)}) custom-call(s32[16,16]{1,0:T(8,128)} %owner_any.1, s32[16]{0:T(128)} %doc_any.1, bf16[128,2048]{1,0:T(8,128)(2,1)} %q_any.1, bf16[128,512]{1,0:T(8,128)(2,1)} %k_any.1, bf16[128,512]{1,0:T(8,128)(2,1)} %v_any.1), custom_call_target="tpu_custom_call" | custom-call | tf_op jit(solution)/shard_map/pack/pallas_call | solution.py:224
  1.6 24.0 %all_to_all.10.data_ref = bf16[16,256,128]{2,1,0:T(8,128)(2,1)S(1)} all-to-all(bf16[16,256,128]{2,1,0:T(8,128)(2,1)S(1)} %get-tuple-element.11), channel_id=1, replica_groups={{10,12,20,22,16,8,14,0,2,30,4,6,26,28,18,24},{11,13,21,23,17,9,15,1,3,3..., dimensions={0} | all-to-all | bytes 2097152 | tf_op jit(solution)/shard_map/all_to_all | solution.py:244
  25.7 1.9 %collective-permute-start = (bf16[16,128,128]{2,1,0:T(8,128)(2,1)S(1)}, bf16[16,128,128]{2,1,0:T(8,128)(2,1)S(1)}, u32[]{:S(2)}, u32[]{:S(2)}) collective-permute-start(bf16[16,128,128]{2,1,0:T(8,128)(2,1)S(1)} %slice.4), channel_id=1, source_target_pairs={{0,2},{2,0},{4,6},{6,4},{8,10},{10,8},{12,14},{14,12},{16,18},{18,... | collective-permute-start | bytes 1572872 | tf_op jit(solution)/shard_map/ppermute | solution.py:245
  27.6 1.8 %own_half.1 = (f32[16,128,128]{2,1,0:T(8,128)S(1)}, f32[16,128]{1,0:T(8,128)S(1)}, f32[16,128]{1,0:T(8,128)S(1)}) custom-call(s32[2,16,128]{2,1,0:T(8,128)S(1)} %get-tuple-element.10.rows_ref, bf16[16,256,128]{2,1,0:T(8,128)(2,1)S(1)} %all_to_all.10.data_ref), custom_call_target="tpu_custom_call" | custom-call | flops 1000000000 | bytes 3145728 | tf_op jit(solution)/shard_map/own_half/pallas_call | solution.py:246
  29.4 0.1 collective-permute-done.other_ref
  29.5 1.9 %other_half.1 = bf16[4,128,512]{2,1,0:T(8,128)(2,1)S(1)} custom-call(s32[2,16,128]{2,1,0:T(8,128)S(1)} %get-tuple-element.10.rows_ref, bf16[16,256,128]{2,1,0:T(8,128)(2,1)S(1)} %all_to_all.10.data_ref, bf16[16,128,128]{2,1,0:T(8,128)(2,1)S(1)} %collective-permute-done.other_ref, f32[16,128,128]{2,1,0:T(8,128)S(1)} %get-tuple-element.12.sums_ref, ...), custom_call_target="tpu_custom_call" | custom-call | tf_op jit(solution)/shard_map/other_half/pallas_call | solution.py:259
  31.3 11.8 %all_to_all.11.in_ref = bf16[4,128,512]{2,1,0:T(8,128)(2,1)S(1)} all-to-all(bf16[4,128,512]{2,1,0:T(8,128)(2,1)S(1)} %other_half.1), channel_id=1, replica_groups={{8,0,12,4},{10,2,14,6},{24,16,28,20},{26,18,30,22},{9,1,13,5},{11,3,15,..., dimensions={0} | all-to-all | bytes 1048576 | tf_op jit(solution)/shard_map/all_to_all | solution.py:269
  43.2 0.8 %unpack.1 = bf16[128,2048]{1,0:T(8,128)(2,1)} custom-call(bf16[4,128,512]{2,1,0:T(8,128)(2,1)S(1)} %all_to_all.11.in_ref), custom_call_target="tpu_custom_call" | custom-call | tf_op jit(solution)/shard_map/unpack/pallas_call | solution.py:270
  (1 shorter events, 0.0 us)
Async XLA Ops:
  25.7 3.8 %collective-permute-start = (bf16[16,128,128]{2,1,0:T(8,128)(2,1)S(1)}, bf16[16,128,128]{2,1,0:T(8,128)(2,1)S(1)}, u32[]{:S(2)}, u32[]{:S(2)}) collective-permute-start(bf16[16,128,128]{2,1,0:T(8,128)(2,1)S(1)} %slice.4), channel_id=1, source_target_pairs={{0,2},{2,0},{4,6},{6,4},{8,10},{10,8},{12,14},{14,12},{16,18},{18,... | collective-permute-start | bytes 1572872 | tf_op jit(solution)/shard_map/ppermute | solution.py:245

commit v8 on v7

--- a/solution.py
+++ b/solution.py
@@ -169,8 +169,9 @@
             total = jnp.sum(totals[i], axis=0, keepdims=True)
             emit(2 * pair + i, mixed[:, i * TOK : (i + 1) * TOK], tops[i], total)
 
-    ahead = scores(0)
-    for pair in range(1, CTX // 2):
+    order = (1, 3, 5, 7, 6, 4, 2, 0)
+    ahead = scores(order[0])
+    for pair in order[1:]:
         following = scores(pair)
         finish(ahead)
         ahead = following

time: 44.2 us -> 43.9 us (level)
  no operation moved by 1% of the time
where the time goes in v8:
time: 43.9 us; the launch traced here: 43.6 us
  blocking collectives  35.6 us (81%)
  Pallas kernels  5.8 us (13%)
  starting transfers between devices  1.92 us (4%)
    all_to_all x1, blocking collectives, body(): lax.all_to_all(packed, 'ctx', 0, 0, tiled=True, axis_index_groups=[ORDER])  24 us
    all_to_all x1, blocking collectives, body(): lax.all_to_all(mixed, 'ctx', 0, 0, tiled=True, axis_index_groups=rings)  11.6 us
    ppermute x1, starting transfers between devices, body(): other = lax.ppermute(data[:, TOK:], 'ctx', [(i, i ^ 1) for i in range(CTX)])  1.92 us
    pallas_call x1, Pallas kernels, body(): pl.pallas_call(other_kernel, out_shape=jax.ShapeDtypeStruct((4, TOK, GROU...  1.77 us
    pallas_call x1, Pallas kernels, body(): pl.pallas_call(own_kernel, out_shape=(jax.ShapeDtypeStruct((CTX, HEAD, TO...  1.66 us
    pallas_call x1, Pallas kernels, body(): pl.pallas_call(pack_kernel, out_shape=(jax.ShapeDtypeStruct((CTX, CHUNK,...  1.56 us
  transfers between devices with their start and end apart: 1, of which 1 were waited for; matrix products, arithmetic and copies ran while one was open for 0% of the time, Pallas kernels for 4%

profile of v8, /device:TPU:1, one launch (start us, length us, event | category | flops | bytes accessed | tf_op | source)
XLA Modules:
  0.0 43.6 jit_solution(13263480111368362311)
XLA Ops:
  0.0 1.6 %pack.1 = (bf16[16,256,128]{2,1,0:T(8,128)(2,1)S(1)}, s32[2,16,128]{2,1,0:T(8,128)S(1)}) custom-call(s32[16,16]{1,0:T(8,128)} %owner_any.1, s32[16]{0:T(128)} %doc_any.1, bf16[128,2048]{1,0:T(8,128)(2,1)} %q_any.1, bf16[128,512]{1,0:T(8,128)(2,1)} %k_any.1, bf16[128,512]{1,0:T(8,128)(2,1)} %v_any.1), custom_call_target="tpu_custom_call" | custom-call | tf_op jit(solution)/shard_map/pack/pallas_call | solution.py:225
  1.6 24.0 %all_to_all.10.data_ref = bf16[16,256,128]{2,1,0:T(8,128)(2,1)S(1)} all-to-all(bf16[16,256,128]{2,1,0:T(8,128)(2,1)S(1)} %get-tuple-element.11), channel_id=1, replica_groups={{10,12,20,22,16,8,14,0,2,30,4,6,26,28,18,24},{11,13,21,23,17,9,15,1,3,3..., dimensions={0} | all-to-all | bytes 2097152 | tf_op jit(solution)/shard_map/all_to_all | solution.py:245
  25.7 1.9 %collective-permute-start = (bf16[16,128,128]{2,1,0:T(8,128)(2,1)S(1)}, bf16[16,128,128]{2,1,0:T(8,128)(2,1)S(1)}, u32[]{:S(2)}, u32[]{:S(2)}) collective-permute-start(bf16[16,128,128]{2,1,0:T(8,128)(2,1)S(1)} %slice.4), channel_id=1, source_target_pairs={{0,2},{2,0},{4,6},{6,4},{8,10},{10,8},{12,14},{14,12},{16,18},{18,... | collective-permute-start | bytes 1572872 | tf_op jit(solution)/shard_map/ppermute | solution.py:246
  27.6 1.7 %own_half.1 = (f32[16,128,128]{2,1,0:T(8,128)S(1)}, f32[16,128]{1,0:T(8,128)S(1)}, f32[16,128]{1,0:T(8,128)S(1)}) custom-call(s32[2,16,128]{2,1,0:T(8,128)S(1)} %get-tuple-element.10.rows_ref, bf16[16,256,128]{2,1,0:T(8,128)(2,1)S(1)} %all_to_all.10.data_ref), custom_call_target="tpu_custom_call" | custom-call | flops 1000000000 | bytes 3145728 | tf_op jit(solution)/shard_map/own_half/pallas_call | solution.py:247
  29.2 0.2 collective-permute-done.other_ref
  29.5 1.8 %other_half.1 = bf16[4,128,512]{2,1,0:T(8,128)(2,1)S(1)} custom-call(s32[2,16,128]{2,1,0:T(8,128)S(1)} %get-tuple-element.10.rows_ref, bf16[16,256,128]{2,1,0:T(8,128)(2,1)S(1)} %all_to_all.10.data_ref, bf16[16,128,128]{2,1,0:T(8,128)(2,1)S(1)} %collective-permute-done.other_ref, f32[16,128,128]{2,1,0:T(8,128)S(1)} %get-tuple-element.12.sums_ref, ...), custom_call_target="tpu_custom_call" | custom-call | tf_op jit(solution)/shard_map/other_half/pallas_call | solution.py:260
  31.2 11.6 %all_to_all.11.in_ref = bf16[4,128,512]{2,1,0:T(8,128)(2,1)S(1)} all-to-all(bf16[4,128,512]{2,1,0:T(8,128)(2,1)S(1)} %other_half.1), channel_id=1, replica_groups={{8,0,12,4},{10,2,14,6},{24,16,28,20},{26,18,30,22},{9,1,13,5},{11,3,15,..., dimensions={0} | all-to-all | bytes 1048576 | tf_op jit(solution)/shard_map/all_to_all | solution.py:270
  42.8 0.8 %unpack.1 = bf16[128,2048]{1,0:T(8,128)(2,1)} custom-call(bf16[4,128,512]{2,1,0:T(8,128)(2,1)S(1)} %all_to_all.11.in_ref), custom_call_target="tpu_custom_call" | custom-call | tf_op jit(solution)/shard_map/unpack/pallas_call | solution.py:271
  (1 shorter events, 0.0 us)
Async XLA Ops:
  25.7 3.8 %collective-permute-start = (bf16[16,128,128]{2,1,0:T(8,128)(2,1)S(1)}, bf16[16,128,128]{2,1,0:T(8,128)(2,1)S(1)}, u32[]{:S(2)}, u32[]{:S(2)}) collective-permute-start(bf16[16,128,128]{2,1,0:T(8,128)(2,1)S(1)} %slice.4), channel_id=1, source_target_pairs={{0,2},{2,0},{4,6},{6,4},{8,10},{10,8},{12,14},{14,12},{16,18},{18,... | collective-permute-start | bytes 1572872 | tf_op jit(solution)/shard_map/ppermute | solution.py:246

commit v9 on v8

--- a/solution.py
+++ b/solution.py
@@ -31,10 +31,9 @@
     return lax.dot_general(a, b, dims, preferred_element_type=jnp.float32)
 
 
-def pack_kernel(owner_any, doc_any, q_any, k_any, v_any, out_ref, rows_ref, owner_ref, owners_ref, doc_ref, q_ref, k_ref, v_ref, sems):
+def pack_kernel(owner_any, doc_any, q_any, k_any, v_any, out_ref, rows_ref, owners_ref, doc_ref, q_ref, k_ref, v_ref, sems):
     me = lax.axis_index("ctx")
     moves = (
-        (owner_any, owner_ref),
         (owner_any, owners_ref),
         (doc_any, doc_ref),
         (k_any, k_ref),
@@ -44,12 +43,13 @@
     copies = [pltpu.make_async_copy(src, dst, sems.at[i]) for i, (src, dst) in enumerate(moves)]
     for copy in copies:
         copy.start()
-    for copy in copies[:3]:
+    for copy in copies[:2]:
         copy.wait()
+    own_row = owners_ref[pl.ds(me, 1), :]
     one_lane = lax.broadcasted_iota(jnp.int32, (1, TOK), 1)
     goal = one_lane % BR
     for b in range(CTX):
-        owner = owner_ref[me, b]
+        owner = own_row[:, b : b + 1]
         rank = ((owner // 8) * 2 + owner % 2) * 4 + (owner // 2) % 4
         goal = goal + jnp.where(one_lane // BR == b, rank * BR, 0)
     row = lax.broadcasted_iota(jnp.int32, (TOK, TOK), 0)
@@ -70,7 +70,7 @@
     rows_ref[0] = pos
     rows_ref[1] = start
 
-    for copy in copies[3:5]:
+    for copy in copies[2:4]:
         copy.wait()
     for g in range(GROUPS):
         cols = slice(g * HEAD, (g + 1) * HEAD)
@@ -81,7 +81,7 @@
             half = slice(part % 2 * 64, part % 2 * 64 + 64)
             out_ref[dest, 128:192, :] = keys[half]
             out_ref[dest, 192:256, :] = vals[half]
-    copies[5].wait()
+    copies[4].wait()
     for g in range(GROUPS):
         wide = slice(g * GROUP_HEADS * HEAD, (g + 1) * GROUP_HEADS * HEAD)
         moved = dot(order, q_ref[:, wide], ROWS_BY_COLS).astype(jnp.bfloat16)
@@ -165,9 +165,12 @@
         mixed = dot(
             jnp.concatenate([turned[m] for m in tiles], 1), jnp.concatenate(wide, 0), ROWS_BY_COLS
         )
-        for i in range(2):
-            total = jnp.sum(totals[i], axis=0, keepdims=True)
-            emit(2 * pair + i, mixed[:, i * TOK : (i + 1) * TOK], tops[i], total)
+        emit(
+            pair,
+            [mixed[:, i * TOK : (i + 1) * TOK] for i in range(2)],
+            tops,
+            [jnp.sum(total, axis=0, keepdims=True) for total in totals],
+        )
 
     order = (1, 3, 5, 7, 6, 4, 2, 0)
     ahead = scores(order[0])
@@ -179,26 +182,31 @@
 
 
 def own_kernel(rows_ref, data_ref, sums_ref, peaks_ref, totals_ref):
-    def emit(s, mixed, top, total):
-        sums_ref[s] = mixed
-        peaks_ref[s : s + 1, :] = top
-        totals_ref[s : s + 1, :] = total
+    def emit(pair, mixed, tops, totals):
+        for i in range(2):
+            s = 2 * pair + i
+            sums_ref[s] = mixed[i]
+            peaks_ref[s : s + 1, :] = tops[i]
+            totals_ref[s : s + 1, :] = totals[i]
 
     attend_half(0, rows_ref, data_ref, data_ref, TOK, None, None, None, emit)
 
 
-def other_kernel(rows_ref, data_ref, other_ref, sums_ref, peaks_ref, totals_ref, out_ref, acc_ref):
-    def emit(s, mixed, top, total):
-        shrink = jnp.exp2(peaks_ref[s : s + 1, :] - top)
-        total = total + totals_ref[s : s + 1, :] * shrink
-        rows = ((mixed + sums_ref[s] * shrink) * (1.0 / total)).T
+def other_kernel(rows_ref, data_ref, other_ref, sums_ref, peaks_ref, totals_ref, out_ref):
+    def emit(pair, mixed, tops, totals):
+        rows = []
+        for i in range(2):
+            s = 2 * pair + i
+            shrink = jnp.exp2(peaks_ref[s : s + 1, :] - tops[i])
+            scale = 1.0 / (totals[i] + totals_ref[s : s + 1, :] * shrink)
+            rows.append((mixed[i] * scale + sums_ref[s] * (shrink * scale)).T)
         for h in range(GROUP_HEADS):
             for y in range(4):
                 at = h * PART + y * BR
-                acc_ref[SPOT[y], s * BR : (s + 1) * BR, h * HEAD : (h + 1) * HEAD] = rows[at : at + BR]
+                both = jnp.concatenate([rows[0][at : at + BR], rows[1][at : at + BR]], 0)
+                out_ref[SPOT[y], pair * 16 : pair * 16 + 16, h * HEAD : (h + 1) * HEAD] = both.astype(jnp.bfloat16)
 
     attend_half(1, rows_ref, data_ref, other_ref, 0, sums_ref, peaks_ref, totals_ref, emit)
-    out_ref[...] = acc_ref[...].astype(jnp.bfloat16)
 
 
 def unpack_kernel(in_ref, out_any, sems):
@@ -231,13 +239,12 @@
         in_specs=[ANY] * 5,
         out_specs=(VMEM, VMEM),
         scratch_shapes=[
-            pltpu.SMEM((CTX, CTX), jnp.int32),
             pltpu.VMEM((CTX, CTX), jnp.int32),
             pltpu.SMEM((NDOC,), jnp.int32),
             pltpu.VMEM(queries.shape, jnp.bfloat16),
             pltpu.VMEM(keys.shape, jnp.bfloat16),
             pltpu.VMEM(values.shape, jnp.bfloat16),
-            pltpu.SemaphoreType.DMA((6,)),
+            pltpu.SemaphoreType.DMA((5,)),
         ],
         compiler_params=pltpu.CompilerParams(vmem_limit_bytes=24 << 20),
         name="pack",
@@ -262,7 +269,6 @@
         out_shape=jax.ShapeDtypeStruct((4, TOK, GROUP_HEADS * HEAD), jnp.bfloat16),
         in_specs=[VMEM] * 6,
         out_specs=VMEM,
-        scratch_shapes=[pltpu.VMEM((4, TOK, GROUP_HEADS * HEAD), jnp.float32)],
         compiler_params=pltpu.CompilerParams(vmem_limit_bytes=40 << 20),
         name="other_half",
     )(rows, data, other, sums, peaks, totals)

time: 43.9 us -> 43.9 us (level)
  no operation moved by 1% of the time
where the time goes in v9:
time: 43.9 us; the launch traced here: 43.6 us
  blocking collectives  35.6 us (81%)
  Pallas kernels  5.77 us (13%)
  starting transfers between devices  1.92 us (4%)
    all_to_all x1, blocking collectives, body(): lax.all_to_all(packed, 'ctx', 0, 0, tiled=True, axis_index_groups=[ORDER])  24 us
    all_to_all x1, blocking collectives, body(): lax.all_to_all(mixed, 'ctx', 0, 0, tiled=True, axis_index_groups=rings)  11.6 us
    ppermute x1, starting transfers between devices, body(): other = lax.ppermute(data[:, TOK:], 'ctx', [(i, i ^ 1) for i in range(CTX)])  1.92 us
    pallas_call x1, Pallas kernels, body(): pl.pallas_call(other_kernel, out_shape=jax.ShapeDtypeStruct((4, TOK, GROU...  1.78 us
    pallas_call x1, Pallas kernels, body(): pl.pallas_call(own_kernel, out_shape=(jax.ShapeDtypeStruct((CTX, HEAD, TO...  1.65 us
    pallas_call x1, Pallas kernels, body(): pl.pallas_call(pack_kernel, out_shape=(jax.ShapeDtypeStruct((CTX, CHUNK,...  1.52 us
  transfers between devices with their start and end apart: 1, of which 1 were waited for; matrix products, arithmetic and copies ran while one was open for 0% of the time, Pallas kernels for 4%

profile of v9, /device:TPU:1, one launch (start us, length us, event | category | flops | bytes accessed | tf_op | source)
XLA Modules:
  0.0 43.6 jit_solution(995451573395364200)
XLA Ops:
  0.0 1.5 %pack.1 = (bf16[16,256,128]{2,1,0:T(8,128)(2,1)S(1)}, s32[2,16,128]{2,1,0:T(8,128)S(1)}) custom-call(s32[16,16]{1,0:T(8,128)} %owner_any.1, s32[16]{0:T(128)} %doc_any.1, bf16[128,2048]{1,0:T(8,128)(2,1)} %q_any.1, bf16[128,512]{1,0:T(8,128)(2,1)} %k_any.1, bf16[128,512]{1,0:T(8,128)(2,1)} %v_any.1), custom_call_target="tpu_custom_call" | custom-call | tf_op jit(solution)/shard_map/pack/pallas_call | solution.py:233
  1.5 24.0 %all_to_all.10.data_ref = bf16[16,256,128]{2,1,0:T(8,128)(2,1)S(1)} all-to-all(bf16[16,256,128]{2,1,0:T(8,128)(2,1)S(1)} %get-tuple-element.11), channel_id=1, replica_groups={{10,12,20,22,16,8,14,0,2,30,4,6,26,28,18,24},{11,13,21,23,17,9,15,1,3,3..., dimensions={0} | all-to-all | bytes 2097152 | tf_op jit(solution)/shard_map/all_to_all | solution.py:252
  25.6 1.9 %collective-permute-start = (bf16[16,128,128]{2,1,0:T(8,128)(2,1)S(1)}, bf16[16,128,128]{2,1,0:T(8,128)(2,1)S(1)}, u32[]{:S(2)}, u32[]{:S(2)}) collective-permute-start(bf16[16,128,128]{2,1,0:T(8,128)(2,1)S(1)} %slice.4), channel_id=1, source_target_pairs={{0,2},{2,0},{4,6},{6,4},{8,10},{10,8},{12,14},{14,12},{16,18},{18,... | collective-permute-start | bytes 1572872 | tf_op jit(solution)/shard_map/ppermute | solution.py:253
  27.5 1.7 %own_half.1 = (f32[16,128,128]{2,1,0:T(8,128)S(1)}, f32[16,128]{1,0:T(8,128)S(1)}, f32[16,128]{1,0:T(8,128)S(1)}) custom-call(s32[2,16,128]{2,1,0:T(8,128)S(1)} %get-tuple-element.10.rows_ref, bf16[16,256,128]{2,1,0:T(8,128)(2,1)S(1)} %all_to_all.10.data_ref), custom_call_target="tpu_custom_call" | custom-call | flops 1000000000 | bytes 3145728 | tf_op jit(solution)/shard_map/own_half/pallas_call | solution.py:254
  29.2 0.2 collective-permute-done.other_ref
  29.4 1.8 %other_half.1 = bf16[4,128,512]{2,1,0:T(8,128)(2,1)S(1)} custom-call(s32[2,16,128]{2,1,0:T(8,128)S(1)} %get-tuple-element.10.rows_ref, bf16[16,256,128]{2,1,0:T(8,128)(2,1)S(1)} %all_to_all.10.data_ref, bf16[16,128,128]{2,1,0:T(8,128)(2,1)S(1)} %collective-permute-done.other_ref, f32[16,128,128]{2,1,0:T(8,128)S(1)} %get-tuple-element.12.sums_ref, ...), custom_call_target="tpu_custom_call" | custom-call | tf_op jit(solution)/shard_map/other_half/pallas_call | solution.py:267
  31.2 11.6 %all_to_all.11.in_ref = bf16[4,128,512]{2,1,0:T(8,128)(2,1)S(1)} all-to-all(bf16[4,128,512]{2,1,0:T(8,128)(2,1)S(1)} %other_half.1), channel_id=1, replica_groups={{8,0,12,4},{10,2,14,6},{24,16,28,20},{26,18,30,22},{9,1,13,5},{11,3,15,..., dimensions={0} | all-to-all | bytes 1048576 | tf_op jit(solution)/shard_map/all_to_all | solution.py:276
  42.8 0.8 %unpack.1 = bf16[128,2048]{1,0:T(8,128)(2,1)} custom-call(bf16[4,128,512]{2,1,0:T(8,128)(2,1)S(1)} %all_to_all.11.in_ref), custom_call_target="tpu_custom_call" | custom-call | tf_op jit(solution)/shard_map/unpack/pallas_call | solution.py:277
  (1 shorter events, 0.0 us)
Async XLA Ops:
  25.6 3.8 %collective-permute-start = (bf16[16,128,128]{2,1,0:T(8,128)(2,1)S(1)}, bf16[16,128,128]{2,1,0:T(8,128)(2,1)S(1)}, u32[]{:S(2)}, u32[]{:S(2)}) collective-permute-start(bf16[16,128,128]{2,1,0:T(8,128)(2,1)S(1)} %slice.4), channel_id=1, source_target_pairs={{0,2},{2,0},{4,6},{6,4},{8,10},{10,8},{12,14},{14,12},{16,18},{18,... | collective-permute-start | bytes 1572872 | tf_op jit(solution)/shard_map/ppermute | solution.py:253
